TPU v7x, 512 devices: a whole 4x8x8 slice. The times are simulated.
512 devices in a mesh: sub: 8 (over y), row: 64 (over z, x, core).
Axes of the slice: x: 4, y: 8, z: 8, core: 2. Of those that a mesh axis runs over, the one named last changes fastest.
Arguments:
- eigen_basis: bfloat16 [8, 48, 3, 128, 16, 128], P('sub', None, None, 'row'), may hold values from -6 to 6
- material: int32 [8, 128, 16, 128], P('sub'), may hold values from 0 to 15
- counts: int32 [8], P('sub'), may hold values from 8 to 48, as said below
- couple: int32 [8, 2], P('sub'), may hold values 0 or 1
- own_rows: int32 [8, 2, 262144], P('sub', None, 'row'), may hold values from 0 to 12287
- send_rows: int32 [8, 2, 262144], P('sub', None, 'row'), may hold values from 0 to 12287
- stiffness: float32 [16], replicated, may hold values from 0.02 to 0.2
Outputs:
- coarse_diag: float32 [8, 48, 48], P('sub')
- coarse_off: float32 [8, 4, 48, 48], P('sub')
Inputs may be any that keep to these rules, and one draw needn't show every extreme that they name: Subdomain i uses its first counts[i] eigenvectors; some subdomain has exactly 48 and some exactly 8. `own_rows`: entries r * 4096 to (r+1) * 4096 - 1 name rows of row shard r in local numbering. `send_rows`: entries r * 4096 to (r+1) * 4096 - 1 name rows of row shard r in local numbering.
All inputs are finite; a program needn't handle non-finite values. No bound on the sum of `couple` on one device may be relied on, other than what follows from the above.
Results may differ from a plain program's by a relative error of at most 0.0029.
Values may be sent and summed in bfloat16 or wider, within the bound.
A program may use at most 64 MiB of HBM per device.

v0:
```python
import math

import jax
import jax.numpy as jnp
from jax import lax
from jax.sharding import PartitionSpec as P

NORMAL_WEIGHT = 3.0


def extended_2(block, sides, width):
    for axis, dim in sides:
        count = lax.axis_size(axis)
        forward = [(i, i + 1) for i in range(count - 1)]
        backward = [(target, source) for source, target in forward]
        low = lax.ppermute(
            lax.slice_in_dim(block, block.shape[dim] - width, None, axis=dim), axis, forward
        )
        high = lax.ppermute(lax.slice_in_dim(block, 0, width, axis=dim), axis, backward)
        block = jnp.concatenate([low, block, high], axis=dim)
    return block


def passed_along(array, axis, by):
    devices = lax.axis_size(axis)
    return lax.ppermute(array, axis, [(i, (i + by) % devices) for i in range(devices)])


def lookup_stiffness(material, stiffness):
    summed = jnp.zeros(material.shape, jnp.float32)
    for level in range(stiffness.shape[0]):
        summed = summed + jnp.where(material == level, stiffness[level], jnp.float32(0.0))
    return summed


def face_term(field, stiff, along):
    length = field.shape[along]
    lower = lax.slice_in_dim(field, 0, length - 1, axis=along)
    upper = lax.slice_in_dim(field, 1, length, axis=along)
    coef = 0.5 * (
        lax.slice_in_dim(stiff, 0, length - 1, axis=along - 2)
        + lax.slice_in_dim(stiff, 1, length, axis=along - 2)
    )
    flux = coef * (upper - lower)
    pad_low = [(0, 0)] * field.ndim
    pad_high = [(0, 0)] * field.ndim
    pad_low[along] = (1, 0)
    pad_high[along] = (0, 1)
    return jnp.pad(flux, pad_low) - jnp.pad(flux, pad_high)


def component_weight(axis):
    return jnp.where(jnp.arange(3) == axis, NORMAL_WEIGHT, 1.0).reshape(1, 3, 1, 1, 1)


def shards(eigen_basis, material, counts, couple, own_rows, send_rows, stiffness):
    columns = eigen_basis.shape[1]
    planes = eigen_basis.shape[3]
    full_planes = material.shape[1]
    rows_sub = 3 * full_planes * eigen_basis.shape[4] * eigen_basis.shape[5]
    slab_len = own_rows.shape[2]
    scale_off = 1.0 / math.sqrt(lax.axis_size("row") * slab_len)
    column_mask = (jnp.arange(columns) < counts[0]).astype(jnp.bfloat16)
    masked = eigen_basis[0] * column_mask[:, None, None, None, None]
    flat_basis = masked.reshape(columns, -1)
    own_slabs = [jnp.take(flat_basis, own_rows[0, offset], axis=1) for offset in range(2)]
    extended = extended_2(masked, (("row", 2),), 1)
    row_index = lax.axis_index("row")
    start = row_index * planes
    padded_mat = jnp.pad(material[0], ((1, 1), (0, 0), (0, 0)))
    mat_ext = lax.dynamic_slice_in_dim(padded_mat, start, planes + 2, 0)
    stiff_ext = lookup_stiffness(mat_ext, stiffness)
    plane_ids = start - 1 + jnp.arange(planes + 2)
    inside = ((plane_ids >= 0) & (plane_ids < full_planes)).astype(jnp.float32)
    field_ext = extended.astype(jnp.float32)
    face_x = 0.5 * (stiff_ext[:-1] + stiff_ext[1:]) * (inside[:-1] * inside[1:])[:, None, None]
    flux_x = face_x * (field_ext[:, :, 1:] - field_ext[:, :, :-1])
    term_x = flux_x[:, :, :-1] - flux_x[:, :, 1:]
    field_in = field_ext[:, :, 1:-1]
    stiff_in = stiff_ext[1:-1]
    summed = component_weight(0) * term_x
    summed = summed + component_weight(1) * face_term(field_in, stiff_in, 3)
    summed = summed + component_weight(2) * face_term(field_in, stiff_in, 4)
    image = summed.astype(jnp.bfloat16)
    flat_image = image.reshape(columns, -1)
    diagonal_part = jnp.dot(flat_basis, flat_image.T, preferred_element_type=jnp.float32)
    send_slabs = [jnp.take(flat_image, send_rows[0, offset], axis=1) for offset in range(2)]
    peer_slabs = []
    for offset in range(2):
        peer_slabs.append(passed_along(send_slabs[offset], "sub", -(offset + 1)))
    products = [
        jnp.dot(own_slabs[offset], peer_slabs[offset].T, preferred_element_type=jnp.float32)
        for offset in range(2)
    ]
    diagonal_sum, pair_first, pair_second = lax.psum(
        (diagonal_part, products[0], products[1]), "row"
    )
    coupling = couple[0].astype(jnp.float32) * scale_off
    forward = [pair_first * coupling[0], pair_second * coupling[1]]
    backward = []
    for offset in range(2):
        backward.append(passed_along(forward[offset].T, "sub", offset + 1))
    coarse_diag = (diagonal_sum * (1.0 / rows_sub))[None]
    coarse_off = jnp.stack([backward[1], backward[0], forward[0], forward[1]], axis=0)[None]
    return (coarse_diag, coarse_off)


def solution(mesh):
    in_specs = (
        P("sub", None, None, "row", None, None),
        P("sub", None, None, None),
        P("sub"),
        P("sub", None),
        P("sub", None, "row"),
        P("sub", None, "row"),
        P(),
    )
    out_specs = (P("sub", None, None), P("sub", None, None, None))
    return jax.shard_map(shards, mesh=mesh, in_specs=in_specs, out_specs=out_specs, check_vma=False)
```

profile of v0, /device:TPU:1, one launch (start us, length us, event | category | flops | bytes accessed | tf_op | source)
XLA Modules:
  0.0 402.2 jit_solution(14822017450566570113)
XLA Ops:
  1.3 1.5 bitcast_multiply_fusion.1
  2.8 1.0 copy-done
  3.8 1.2 fusion.31
  5.1 4.5 %collective-permute-start = (bf16[48,3,1,16,128]{4,3,2,1,0:T(8,128)(2,1)}, bf16[48,3,1,16,128]{4,3,2,1,0:T(8,128)(2,1)}, u32[]{:S(2)}, u32[]{:S(2)}) collective-permute-start(bf16[48,3,1,16,128]{4,3,2,1,0:T(8,128)(2,1)} %get-tuple-element.6), channel_id=1, source_target_pairs={{0,1},{1,2},{2,3},{3,4},{4,5},{5,6},{6,7},{7,8},{8,9},{9,10},{10,1... | collective-permute-start | bytes 1769480 | tf_op jit(solution)/shard_map/ppermute | solution.py:16
  9.6 6.4 %collective-permute-start.1 = (bf16[48,3,1,16,128]{4,3,2,1,0:T(8,128)(2,1)}, bf16[48,3,1,16,128]{4,3,2,1,0:T(8,128)(2,1)}, u32[]{:S(2)}, u32[]{:S(2)}) collective-permute-start(bf16[48,3,1,16,128]{4,3,2,1,0:T(8,128)(2,1)} %get-tuple-element.7), channel_id=1, source_target_pairs={{1,0},{2,1},{3,2},{4,3},{5,4},{6,5},{7,6},{8,7},{9,8},{10,9},{11,1... | collective-permute-start | bytes 1769480 | tf_op jit(solution)/shard_map/ppermute | solution.py:19
  16.0 0.7 fusion.35
  16.7 10.1 %select_add_fusion = f32[4,16,128]{2,1,0:T(8,128)S(1)} fusion(s32[]{:T(128)S(6)} %select_n.82, s32[128,16,128]{2,1,0:T(8,128)S(1)} %bitcast.62, f32[]{:T(128)} %bitcast.18, f32[]{:T(128)} %bitcast.17, f32[]{:T(128)} %bitcast.16, f32[]{:T(128)} %bitcast.15, f32[]{:T(128)} %bitcast.14, f32[]{:T(128)} %bitcast.13, f32[]{:T(128)} %bitcast.12, f32[]{:T(128)} %bitcast.11, ...), kind=kLoop, calls=%fused_computation.39 | loop fusion | flops 385024 | bytes 1081412 | tf_op jit(solution)/shard_map/add | solution.py:32
  27.0 3.0 copy.17
  31.4 2.0 bitcast_multiply_fusion
  34.0 14.9 %gather_fusion.2 = bf16[4096,48]{1,0:T(8,128)(2,1)} fusion(bf16[48,12288]{0,1:T(8,128)(2,1)S(1)} %bitcast_multiply_fusion, s32[4096]{0:T(1024)S(1)} %fusion.27), kind=kCustom, calls=%fused_computation.2.clone | custom fusion | bytes 802816 | tf_op jit(solution)/shard_map/jit(_take)/gather | solution.py:66
  48.9 14.9 %gather_fusion = bf16[4096,48]{1,0:T(8,128)(2,1)} fusion(bf16[48,12288]{0,1:T(8,128)(2,1)S(1)} %bitcast_multiply_fusion, s32[4096]{0:T(1024)S(1)} %fusion.25), kind=kCustom, calls=%fused_computation.clone | custom fusion | bytes 802816 | tf_op jit(solution)/shard_map/jit(_take)/gather | solution.py:66
  64.6 1.9 maximum_convert_fusion
  68.2 2.3 fusion.6
  70.5 3.2 copy.18
  73.7 14.9 %gather_fusion.3 = bf16[4096,48]{1,0:T(8,128)(2,1)} fusion(bf16[48,12288]{0,1:T(8,128)(2,1)S(1)} %bitcast.60, s32[4096]{0:T(1024)S(1)} %fusion.28), kind=kCustom, calls=%fused_computation.3.clone | custom fusion | bytes 802816 | tf_op jit(solution)/shard_map/jit(_take)/gather | solution.py:87
  88.6 4.2 %select_bitcast_fusion = bf16[48,4096]{0,1:T(8,128)(2,1)} fusion(bf16[4096,48]{1,0:T(8,128)(2,1)} %gather_fusion.3, pred[4096]{0:T(1024)(128)(4,1)S(1)} %compare_and_fusion), kind=kLoop, calls=%fused_computation.26 | loop fusion | flops 196608 | bytes 790528 | tf_op jit(solution)/shard_map/jit(_take)/select_n | solution.py:87
  92.8 1.5 copy.21
  94.4 1.9 collective-permute-start.4
  96.3 14.9 %gather_fusion.1 = bf16[4096,48]{1,0:T(8,128)(2,1)} fusion(bf16[48,12288]{0,1:T(8,128)(2,1)S(1)} %bitcast.61, s32[4096]{0:T(1024)S(1)} %fusion.26), kind=kCustom, calls=%fused_computation.1.clone | custom fusion | bytes 802816 | tf_op jit(solution)/shard_map/jit(_take)/gather | solution.py:87
  111.2 4.1 %select_bitcast_fusion.1 = bf16[48,4096]{0,1:T(8,128)(2,1)} fusion(bf16[4096,48]{1,0:T(8,128)(2,1)} %gather_fusion.1, pred[4096]{0:T(1024)(128)(4,1)} %compare_and_fusion.2), kind=kLoop, calls=%fused_computation.28 | loop fusion | flops 196608 | bytes 790528 | tf_op jit(solution)/shard_map/jit(_take)/select_n | solution.py:87
  115.3 2.3 copy.19
  117.6 2.6 collective-permute-start.2
  120.2 2.6 fusion.9
  122.9 2.0 fusion.12
  124.9 15.3 %collective-permute-done.2 = bf16[48,4096]{1,0:T(8,128)(2,1)S(1)} collective-permute-done((bf16[48,4096]{1,0:T(8,128)(2,1)}, bf16[48,4096]{1,0:T(8,128)(2,1)S(1)}, u32[]{:S(2)}, u32[]{:S(2)}) %collective-permute-start.2) | collective-permute-done | bytes 393248 | tf_op jit(solution)/shard_map/ppermute | solution.py:26
  140.1 1.0 fusion.14
  141.2 247.3 %all-reduce.5 = (f32[48,48]{1,0:T(8,128)S(1)}, f32[48,48]{1,0:T(8,128)S(1)}, f32[48,48]{1,0:T(8,128)S(1)}) all-reduce(f32[48,48]{1,0:T(8,128)S(1)} %copy-done.6, f32[48,48]{1,0:T(8,128)S(1)} %fusion.14, f32[48,48]{1,0:T(8,128)S(1)} %fusion.12), channel_id=1, replica_groups=mesh['sub'=8,'row'=64] {'row'}, use_global_device_ids=true, to_apply=%region_0.1 | all-reduce | flops 6912 | bytes 55296 | tf_op jit(solution)/shard_map/psum | solution.py:95
  389.2 0.7 fusion.39
  390.4 3.7 collective-permute-start.5
  394.3 2.1 collective-permute-start.3
  397.0 1.4 collective-permute-done.5
  398.5 3.1 collective-permute-done.3
  (55 shorter events, 7.2 us)
Async XLA Ops:
  1.3 14.7 %copy-start.5 = (f32[16]{0:T(128)S(1)}, f32[16]{0:T(128)}, u32[]{:S(2)}) copy-start(f32[16]{0:T(128)} %param.15) | copy-start | bytes 196
  1.3 15.4 %copy-start.2 = (s32[1,128,16,128]{3,2,1,0:T(8,128)S(1)}, s32[1,128,16,128]{3,2,1,0:T(8,128)}, u32[]{:S(2)}) copy-start(s32[1,128,16,128]{3,2,1,0:T(8,128)} %param.10) | copy-start | bytes 3145732
  2.8 1.0 copy-start
  3.8 23.1 %copy-start.7 = (s32[1,2,4096]{2,1,0:T(2,128)S(1)}, s32[1,2,4096]{2,1,0:T(2,128)}, u32[]{:S(2)}) copy-start(s32[1,2,4096]{2,1,0:T(2,128)} %param.14) | copy-start | bytes 98308
  3.8 23.2 %copy-start.1 = (bf16[1,48,3,2,16,128]{5,4,3,2,1,0:T(8,128)(2,1)S(1)}, bf16[1,48,3,2,16,128]{5,4,3,2,1,0:T(8,128)(2,1)}, u32[]{:S(2)}) copy-start(bf16[1,48,3,2,16,128]{5,4,3,2,1,0:T(8,128)(2,1)} %param.9) | copy-start | bytes 3538948
  5.1 59.5 %collective-permute-start = (bf16[48,3,1,16,128]{4,3,2,1,0:T(8,128)(2,1)}, bf16[48,3,1,16,128]{4,3,2,1,0:T(8,128)(2,1)}, u32[]{:S(2)}, u32[]{:S(2)}) collective-permute-start(bf16[48,3,1,16,128]{4,3,2,1,0:T(8,128)(2,1)} %get-tuple-element.6), channel_id=1, source_target_pairs={{0,1},{1,2},{2,3},{3,4},{4,5},{5,6},{6,7},{7,8},{8,9},{9,10},{10,1... | collective-permute-start | bytes 1769480 | tf_op jit(solution)/shard_map/ppermute | solution.py:16
  9.6 55.0 %collective-permute-start.1 = (bf16[48,3,1,16,128]{4,3,2,1,0:T(8,128)(2,1)}, bf16[48,3,1,16,128]{4,3,2,1,0:T(8,128)(2,1)}, u32[]{:S(2)}, u32[]{:S(2)}) collective-permute-start(bf16[48,3,1,16,128]{4,3,2,1,0:T(8,128)(2,1)} %get-tuple-element.7), channel_id=1, source_target_pairs={{1,0},{2,1},{3,2},{4,3},{5,4},{6,5},{7,6},{8,7},{9,8},{10,9},{11,1... | collective-permute-start | bytes 1769480 | tf_op jit(solution)/shard_map/ppermute | solution.py:19
  26.8 3.2 copy-start.8
  31.4 2.6 copy-start.11
  94.4 28.5 %collective-permute-start.4 = (bf16[48,4096]{1,0:T(8,128)(2,1)S(1)}, bf16[48,4096]{1,0:T(8,128)(2,1)}, u32[]{:S(2)}, u32[]{:S(2)}) collective-permute-start(bf16[48,4096]{1,0:T(8,128)(2,1)S(1)} %copy.21), channel_id=1, source_target_pairs={{0,448},{64,0},{128,64},{192,128},{256,192},{320,256},{384,320},{4... | collective-permute-start | bytes 1179656 | tf_op jit(solution)/shard_map/ppermute | solution.py:26
  117.6 5.3 %copy-start.4 = (bf16[4096,48]{1,0:T(8,128)(2,1)S(1)}, bf16[4096,48]{1,0:T(8,128)(2,1)}, u32[]{:S(2)}) copy-start(bf16[4096,48]{1,0:T(8,128)(2,1)} %gather_fusion.2) | copy-start | bytes 1179652
  117.6 5.3 %copy-start.10 = (pred[4096]{0:T(1024)(128)(4,1)S(1)}, pred[4096]{0:T(1024)(128)(4,1)}, u32[]{:S(2)}) copy-start(pred[4096]{0:T(1024)(128)(4,1)} %compare_and_fusion.1) | copy-start | bytes 12292
  117.6 22.5 %copy-start.3 = (bf16[4096,48]{1,0:T(8,128)(2,1)S(1)}, bf16[4096,48]{1,0:T(8,128)(2,1)}, u32[]{:S(2)}) copy-start(bf16[4096,48]{1,0:T(8,128)(2,1)} %gather_fusion) | copy-start | bytes 1179652
  117.6 22.5 %copy-start.9 = (pred[4096]{0:T(1024)(128)(4,1)S(1)}, pred[4096]{0:T(1024)(128)(4,1)}, u32[]{:S(2)}) copy-start(pred[4096]{0:T(1024)(128)(4,1)} %compare_and_fusion.3) | copy-start | bytes 12292
  117.6 22.5 %collective-permute-start.2 = (bf16[48,4096]{1,0:T(8,128)(2,1)}, bf16[48,4096]{1,0:T(8,128)(2,1)S(1)}, u32[]{:S(2)}, u32[]{:S(2)}) collective-permute-start(bf16[48,4096]{1,0:T(8,128)(2,1)} %copy.19), channel_id=1, source_target_pairs={{0,384},{64,448},{128,0},{192,64},{256,128},{320,192},{384,256},{4... | collective-permute-start | bytes 1179656 | tf_op jit(solution)/shard_map/ppermute | solution.py:26
  122.9 18.3 %copy-start.6 = (f32[48,48]{1,0:T(8,128)S(1)}, f32[48,48]{1,0:T(8,128)}, u32[]{:S(2)}) copy-start(f32[48,48]{1,0:T(8,128)} %fusion.9) | copy-start | bytes 27652
  390.4 8.0 %collective-permute-start.5 = (f32[48,48]{0,1:T(8,128)S(1)}, f32[48,48]{0,1:T(8,128)S(1)}, u32[]{:S(2)}, u32[]{:S(2)}) collective-permute-start(f32[48,48]{0,1:T(8,128)S(1)} %get-tuple-element.12), channel_id=1, source_target_pairs={{0,64},{64,128},{128,192},{192,256},{256,320},{320,384},{384,448},... | collective-permute-start | bytes 27656 | tf_op jit(solution)/shard_map/ppermute | solution.py:26
  394.3 7.3 %collective-permute-start.3 = (f32[48,48]{1,0:T(8,128)S(1)}, f32[48,48]{1,0:T(8,128)S(1)}, u32[]{:S(2)}, u32[]{:S(2)}) collective-permute-start(f32[48,48]{1,0:T(8,128)S(1)} %bitcast.73), channel_id=1, source_target_pairs={{0,128},{64,192},{128,256},{192,320},{256,384},{320,448},{384,0},{... | collective-permute-start | bytes 27656 | tf_op jit(solution)/shard_map/ppermute | solution.py:26
where the time goes:
time: 407 us; the launch traced here: 402 us
  blocking collectives  247 us (61%)
  local copies, waits for them, and re-layouts  73.6 us (18%)
  other arithmetic  33.1 us (8%)
  starting transfers between devices  21.3 us (5%)
  waiting for transfers between devices  19.8 us (5%)
  matrix products  5.6 us (1%)
    psum x1, blocking collectives, shards(): lax.psum((diagonal_part, products[0], products[1]), 'row')  247 us
    gather x2, local copies, waits for them, and re-layouts, shards(): jnp.take(flat_image, send_rows[0, offset], axis=1)  29.8 us
    gather x2, local copies, waits for them, and re-layouts, shards(): jnp.take(flat_basis, own_rows[0, offset], axis=1)  29.8 us
    ppermute x4, waiting for transfers between devices, passed_along(): lax.ppermute(array, axis, [(i, (i + by) % devices) for i in range(devices)])  19.8 us
    ppermute x4, starting transfers between devices, passed_along(): lax.ppermute(array, axis, [(i, (i + by) % devices) for i in range(devices)])  10.4 us
    add x1, other arithmetic, lookup_stiffness(): summed + jnp.where(material == level, stiffness[level], jnp.float32(0.0))  10.1 us
    select_n x2, other arithmetic, shards(): jnp.take(flat_image, send_rows[0, offset], axis=1)  8.28 us
  transfers between devices with their start and end apart: 6, of which 3 were waited for; matrix products, arithmetic and copies ran while one was open for 19% of the time, Pallas kernels for 0%

commit v1 on v0

v1 whole, which is shorter than its diff:
```python
import functools
import math

import jax
import jax.numpy as jnp
from jax import lax
from jax.experimental import pallas as pl
from jax.experimental.pallas import tpu as pltpu
from jax.sharding import PartitionSpec as P

MESH = pl.DeviceIdType.MESH
F32 = jnp.float32
BF16 = jnp.bfloat16

K = 48
C = 3
CX = 2
GY = 16
GZ = 128
CELLS = CX * GY * GZ
ROWS = C * CELLS
NSUB = 8
NROW = 64
PLANES = NROW * CX
SLAB = 4096
CHUNK = 1024
NCHUNK = SLAB // CHUNK
NLEVEL = 16
GROUP = 8
OWNERS = 6
LANES = 128
UNROLL = 128


def at_sub(sub, by):
    return lax.rem(sub + (by + NSUB), NSUB)


def start_barrier(sub, row):
    z, place = row // GROUP, lax.rem(row, GROUP)
    barrier = pltpu.get_barrier_semaphore()

    def signal(to_sub, to_row):
        pl.semaphore_signal(barrier, inc=1, device_id=(to_sub, to_row), device_id_type=MESH)

    @pl.when(row > 0)
    def _():
        signal(sub, row - 1)

    @pl.when(row < NROW - 1)
    def _():
        signal(sub, row + 1)

    for by in (1, 2):
        signal(at_sub(sub, -by), row)
        for q in range(OWNERS):
            signal(at_sub(sub, by), z * GROUP + q)
    for step in range(1, GROUP):
        signal(sub, z * GROUP + lax.rem(place + step, GROUP))

    @pl.when(place < OWNERS)
    def _():
        for step in range(1, 8):
            signal(sub, lax.rem(z + step, 8) * GROUP + place)

    owner = (place < OWNERS).astype(jnp.int32)
    sides = (row > 0).astype(jnp.int32) + (row < NROW - 1).astype(jnp.int32)
    return barrier, sides + 2 + (GROUP - 1) + owner * (7 + 2 * GROUP)


def gather(index_of, table, dest, first, count):
    def body(step, carry):
        base = pl.multiple_of(step * UNROLL, UNROLL)
        for u in range(UNROLL):
            dest[pl.ds(base + u, 1), :] = table[pl.ds(index_of(first + base + u), 1), :]
        return carry

    lax.fori_loop(0, count // UNROLL, body, 0)


def widen(tile):
    return jnp.concatenate([tile, jnp.zeros((GZ, LANES - K), F32)], axis=1)


def kernel(
    counts, couple, stiffness, eigen, material, own_rows, send_rows,
    diag_out, off_out,
    eig, halo, mat, coef, field, image, table, own_sel, send_sel, packed, arrived,
    own_index, send_index, part, sums, zsums, piece, whole, forward,
    load_sem, halo_send, halo_recv, slab_send, slab_recv,
    one_send, one_recv, two_send, two_recv, three_send, three_recv, fwd_send, fwd_recv,
):
    sub, row = lax.axis_index("sub"), lax.axis_index("row")
    z, place = row // GROUP, lax.rem(row, GROUP)
    barrier, greetings = start_barrier(sub, row)

    loads = [pltpu.make_async_copy(eigen.at[0], eig, load_sem.at[0])]
    loads.append(pltpu.make_async_copy(own_rows, own_index, load_sem.at[1]))
    loads.append(pltpu.make_async_copy(send_rows, send_index, load_sem.at[2]))
    for p in range(CX + 2):
        plane = jnp.clip(row * CX + (p - 1), 0, PLANES - 1)
        loads.append(pltpu.make_async_copy(material.at[0, plane], mat.at[p], load_sem.at[3 + p]))
    for load in loads:
        load.start()

    count = counts[0]

    def kept(k):
        return (k < count).astype(F32)

    loads[0].wait()

    pl.semaphore_wait(barrier, greetings)
    up = pltpu.make_async_remote_copy(
        src_ref=eig.at[:, :, CX - 1], dst_ref=halo.at[0], send_sem=halo_send.at[0],
        recv_sem=halo_recv.at[0], device_id=(sub, jnp.minimum(row + 1, NROW - 1)), device_id_type=MESH)
    down = pltpu.make_async_remote_copy(
        src_ref=eig.at[:, :, 0], dst_ref=halo.at[1], send_sem=halo_send.at[1],
        recv_sem=halo_recv.at[1], device_id=(sub, jnp.maximum(row - 1, 0)), device_id_type=MESH)

    @pl.when(row < NROW - 1)
    def _():
        up.start()

    @pl.when(row > 0)
    def _():
        down.start()

    @pl.when(row == 0)
    def _():
        halo[0] = jnp.zeros((K, C, GY, GZ), BF16)

    @pl.when(row == NROW - 1)
    def _():
        halo[1] = jnp.zeros((K, C, GY, GZ), BF16)

    def mask_column(k, carry):
        keep = kept(k)
        for c in range(C):
            for p in range(CX):
                base = pl.multiple_of(k * (C * CX * GY) + (c * CX + p) * GY, GY)
                field[pl.ds(base, GY), :] = eig[k, c, p].astype(F32) * keep
        return carry

    lax.fori_loop(0, K, mask_column, 0)

    def across(source, at):
        return source[pl.ds(at, K, stride=C * CX * GY), :]

    def fill_table(at, carry):
        table[pl.ds(pl.multiple_of(at * GZ, GZ), GZ), :] = widen(across(field, at).T)
        return carry

    lax.fori_loop(0, C * CX * GY, fill_table, 0)

    loads[1].wait()
    lane = lax.broadcasted_iota(jnp.int32, (K, LANES), 1)
    line = lax.broadcasted_iota(jnp.int32, (K, LANES), 0)
    slabs = []
    for o in (1, 0):
        turn = jnp.where(lane == line, couple[0, o].astype(F32), F32(0)).astype(BF16)
        for n in range(NCHUNK):
            gather(lambda t: own_index[0, o, t], table, own_sel, n * CHUNK, CHUNK)

            def turned(step, carry):
                base = pl.multiple_of(step * 256, 256)
                picked = own_sel[pl.ds(base, 256), :].astype(BF16)
                packed[o, n, :, pl.ds(base, 256)] = lax.dot_general(
                    turn, picked, (((1,), (1,)), ((), ())), preferred_element_type=F32).astype(BF16)
                return carry

            lax.fori_loop(0, CHUNK // 256, turned, 0)
            slab = pltpu.make_async_remote_copy(
                src_ref=packed.at[o, n], dst_ref=arrived.at[o, n],
                send_sem=slab_send.at[o, n], recv_sem=slab_recv.at[o, n],
                device_id=(at_sub(sub, o + 1), row), device_id_type=MESH)
            slab.start()
            slabs.append(slab)

    for p in range(CX + 2):
        loads[3 + p].wait()
    kappa = []
    for p in range(CX + 2):
        level = mat[p]
        found = jnp.zeros((GY, GZ), F32)
        for m in range(NLEVEL):
            found = found + jnp.where(level == m, stiffness[m], F32(0))
        kappa.append(found)
    for p in range(CX + 1):
        face = 0.5 * (kappa[p] + kappa[p + 1])
        if p == 0:
            face = face * (row > 0).astype(F32)
        if p == CX:
            face = face * (row < NROW - 1).astype(F32)
        coef[p] = face
    in_y = lax.broadcasted_iota(jnp.int32, (GY, GZ), 0) < GY - 1
    in_z = lax.broadcasted_iota(jnp.int32, (GY, GZ), 1) < GZ - 1
    for p in range(CX):
        mid = kappa[p + 1]
        coef[CX + 1 + p] = jnp.where(in_y, 0.5 * (mid + pltpu.roll(mid, GY - 1, 0)), 0.0)
        coef[2 * CX + 1 + p] = jnp.where(in_z, 0.5 * (mid + pltpu.roll(mid, GZ - 1, 1)), 0.0)

    @pl.when(row > 0)
    def _():
        up.wait_recv()

    @pl.when(row < NROW - 1)
    def _():
        down.wait_recv()

    def apply_column(k, carry):
        keep = kept(k)
        for c in range(C):
            def at(p):
                return pl.multiple_of(k * (C * CX * GY) + (c * CX + p) * GY, GY)

            cells = [halo[0, k, c].astype(F32) * keep]
            cells += [field[pl.ds(at(p), GY), :] for p in range(CX)]
            cells.append(halo[1, k, c].astype(F32) * keep)
            flux = [coef[p] * (cells[p + 1] - cells[p]) for p in range(CX + 1)]
            for p in range(CX):
                u = cells[p + 1]
                term_x = flux[p] - flux[p + 1]
                flux_y = coef[CX + 1 + p] * (pltpu.roll(u, GY - 1, 0) - u)
                term_y = pltpu.roll(flux_y, 1, 0) - flux_y
                flux_z = coef[2 * CX + 1 + p] * (pltpu.roll(u, GZ - 1, 1) - u)
                term_z = pltpu.roll(flux_z, 1, 1) - flux_z
                terms = [term_x, term_y, term_z]
                terms[c] = 3.0 * terms[c]
                total = terms[0] + terms[1] + terms[2]
                image[pl.ds(at(p), GY), :] = total.astype(BF16).astype(F32)
        return carry

    lax.fori_loop(0, K, apply_column, 0)

    def image_table(at, total):
        turned = widen(across(image, at).T)
        table[pl.ds(pl.multiple_of(at * GZ, GZ), GZ), :] = turned
        return total + jnp.dot(
            across(field, at).astype(BF16), turned.astype(BF16), preferred_element_type=F32)

    diag = lax.fori_loop(0, C * CX * GY, image_table, jnp.zeros((K, LANES), F32))

    loads[2].wait()
    for o in (1, 0):
        gather(lambda t: send_index[0, o, t], table, send_sel.at[o], 0, SLAB)

    mats = [diag]
    for o in (0, 1):
        for n in range(NCHUNK):
            slabs[(1 - o) * NCHUNK + n].wait_recv()

        def multiply(step, total, o=o):
            n = step
            picked = send_sel[o, pl.ds(pl.multiple_of(n * CHUNK, CHUNK), CHUNK), :].astype(BF16)
            return total + jnp.dot(arrived[o, n], picked, preferred_element_type=F32)

        mats.append(lax.fori_loop(0, NCHUNK, multiply, jnp.zeros((K, LANES), F32)))
    for q in range(OWNERS):
        for m in range(3):
            part[q, pl.ds(8 * m, 8), :] = mats[m][8 * q : 8 * q + 8]

    is_owner = place < OWNERS
    firsts = []
    for step in range(1, GROUP):
        to = lax.rem(place + step, GROUP)
        to_q = jnp.minimum(to, OWNERS - 1)
        firsts.append((to, pltpu.make_async_remote_copy(
            src_ref=part.at[to_q], dst_ref=sums.at[place],
            send_sem=one_send.at[step], recv_sem=one_recv.at[place],
            device_id=(sub, z * GROUP + to), device_id_type=MESH)))
    for to, copy in firsts:
        @pl.when(to < OWNERS)
        def _(copy=copy):
            copy.start()

    seconds = []
    for step in range(1, 8):
        seconds.append(pltpu.make_async_remote_copy(
            src_ref=piece.at[0], dst_ref=zsums.at[z],
            send_sem=two_send.at[step], recv_sem=two_recv.at[z],
            device_id=(sub, lax.rem(z + step, 8) * GROUP + place), device_id_type=MESH))

    thirds = []
    own_q = jnp.minimum(place, OWNERS - 1)
    for step in range(1, GROUP):
        thirds.append(pltpu.make_async_remote_copy(
            src_ref=piece.at[1], dst_ref=whole.at[own_q],
            send_sem=three_send.at[step], recv_sem=three_recv.at[own_q],
            device_id=(sub, z * GROUP + lax.rem(place + step, GROUP)), device_id_type=MESH))
    for o in (0, 1):
        for to in range(GROUP):
            thirds.append(pltpu.make_async_remote_copy(
                src_ref=piece.at[1, pl.ds(8 + 8 * o, 8)], dst_ref=forward.at[o, own_q],
                send_sem=fwd_send.at[o, to], recv_sem=fwd_recv.at[o, own_q],
                device_id=(at_sub(sub, -o - 1), z * GROUP + to), device_id_type=MESH))

    @pl.when(is_owner)
    def _():
        for step in range(1, GROUP):
            source = lax.rem(place + step, GROUP)
            pltpu.make_async_remote_copy(
                src_ref=part.at[0], dst_ref=sums.at[source], send_sem=one_send.at[step],
                recv_sem=one_recv.at[source], device_id=(sub, row), device_id_type=MESH).wait_recv()
        total = part[own_q]
        for step in range(1, GROUP):
            total = total + sums[lax.rem(place + step, GROUP)]
        piece[0] = total
        for copy in seconds:
            copy.start()
        for step in range(1, 8):
            source = lax.rem(z + step, 8)
            pltpu.make_async_remote_copy(
                src_ref=piece.at[0], dst_ref=zsums.at[source], send_sem=two_send.at[step],
                recv_sem=two_recv.at[source], device_id=(sub, row), device_id_type=MESH).wait_recv()
        for step in range(1, 8):
            total = total + zsums[lax.rem(z + step, 8)]
        piece[1] = total
        for copy in thirds:
            copy.start()
        whole[own_q] = total

    for q in range(OWNERS):
        @pl.when(place != q)
        def _(q=q):
            pltpu.make_async_remote_copy(
                src_ref=piece.at[1], dst_ref=whole.at[q], send_sem=three_send.at[0],
                recv_sem=three_recv.at[q], device_id=(sub, row), device_id_type=MESH).wait_recv()
        for o in (0, 1):
            pltpu.make_async_remote_copy(
                src_ref=piece.at[1, pl.ds(8, 8)], dst_ref=forward.at[o, q], send_sem=fwd_send.at[o, q],
                recv_sem=fwd_recv.at[o, q], device_id=(sub, row), device_id_type=MESH).wait_recv()

    scale = 1.0 / math.sqrt(NROW * SLAB)
    diag_out[0] = jnp.concatenate([whole[q, 0:8, :K] for q in range(OWNERS)], axis=0) * (1.0 / (C * PLANES * GY * GZ))
    for o in (0, 1):
        pair = jnp.concatenate([whole[q, 8 + 8 * o : 16 + 8 * o, :] for q in range(OWNERS)], axis=0)
        off_out[0, 1 - o] = pair.T[:K, :] * scale
        off_out[0, 2 + o] = jnp.concatenate([forward[o, q, :, :K] for q in range(OWNERS)], axis=0) * scale

    @pl.when(row < NROW - 1)
    def _():
        up.wait_send()

    @pl.when(row > 0)
    def _():
        down.wait_send()

    for slab in slabs:
        slab.wait_send()
    for to, copy in firsts:
        @pl.when(to < OWNERS)
        def _(copy=copy):
            copy.wait_send()

    @pl.when(is_owner)
    def _():
        for copy in seconds + thirds:
            copy.wait_send()


def shards(eigen_basis, material, counts, couple, own_rows, send_rows, stiffness):
    smem = pl.BlockSpec(memory_space=pltpu.SMEM)
    anywhere = pl.BlockSpec(memory_space=pl.ANY)
    vmem = pl.BlockSpec(memory_space=pltpu.VMEM)
    dma = pltpu.SemaphoreType.DMA
    return pl.pallas_call(
        kernel,
        out_shape=(jax.ShapeDtypeStruct((1, K, K), F32), jax.ShapeDtypeStruct((1, 4, K, K), F32)),
        in_specs=[smem, smem, smem, anywhere, anywhere, anywhere, anywhere],
        out_specs=(vmem, vmem),
        scratch_shapes=[
            pltpu.VMEM((K, C, CX, GY, GZ), BF16),
            pltpu.VMEM((2, K, C, GY, GZ), BF16),
            pltpu.VMEM((CX + 2, GY, GZ), jnp.int32),
            pltpu.VMEM((3 * CX + 1, GY, GZ), F32),
            pltpu.VMEM((K * C * CX * GY, GZ), F32),
            pltpu.VMEM((K * C * CX * GY, GZ), F32),
            pltpu.VMEM((ROWS, LANES), F32),
            pltpu.VMEM((CHUNK, LANES), F32),
            pltpu.VMEM((2, SLAB, LANES), F32),
            pltpu.VMEM((2, NCHUNK, K, CHUNK), BF16),
            pltpu.VMEM((2, NCHUNK, K, CHUNK), BF16),
            pltpu.SMEM((1, 2, SLAB), jnp.int32),
            pltpu.SMEM((1, 2, SLAB), jnp.int32),
            pltpu.VMEM((OWNERS, 24, LANES), F32),
            pltpu.VMEM((GROUP, 24, LANES), F32),
            pltpu.VMEM((8, 24, LANES), F32),
            pltpu.VMEM((2, 24, LANES), F32),
            pltpu.VMEM((OWNERS, 24, LANES), F32),
            pltpu.VMEM((2, OWNERS, 8, LANES), F32),
            dma((3 + CX + 2,)), dma((2,)), dma((2,)), dma((2, NCHUNK)), dma((2, NCHUNK)),
            dma((GROUP,)), dma((GROUP,)), dma((8,)), dma((8,)),
            dma((GROUP,)), dma((OWNERS,)), dma((2, GROUP)), dma((2, OWNERS)),
        ],
        compiler_params=pltpu.CompilerParams(
            collective_id=0, has_side_effects=True, vmem_limit_bytes=48 * 2**20),
        name="coarse",
    )(counts, couple, stiffness, eigen_basis, material, own_rows, send_rows)


def solution(mesh):
    in_specs = (
        P("sub", None, None, "row", None, None),
        P("sub", None, None, None),
        P("sub"),
        P("sub", None),
        P("sub", None, "row"),
        P("sub", None, "row"),
        P(),
    )
    out_specs = (P("sub", None, None), P("sub", None, None, None))
    return jax.shard_map(shards, mesh=mesh, in_specs=in_specs, out_specs=out_specs, check_vma=False)
```

time: 407 us -> 120 us (0.29); the launches traced: 402 us -> 120 us
  blocking collectives: 247 us -> 0 us
  Pallas kernels: 0 us -> 112 us
  local copies, waits for them, and re-layouts: 73.6 us -> 6.56 us
  other arithmetic: 33.1 us -> 0 us
  starting transfers between devices: 21.3 us -> 0 us
  waiting for transfers between devices: 19.8 us -> 0 us
  matrix products: 5.6 us -> 0 us
    psum x1 -> x0, blocking collectives: 247 us -> none  [shards(): lax.psum((diagonal_part, products[0], products[1]), 'row')]
    pallas_call x0 -> x1, Pallas kernels: none -> 112 us  [shards(): pl.pallas_call(kernel, out_shape=(jax.ShapeDtypeStruct((1, K, K), F32), j...]
    gather x4 -> x0, local copies, waits for them, and re-layouts: 59.6 us -> none  [the longest x2 29.8 us: shards(): jnp.take(flat_image, send_rows[0, offset], axis=1)]
    ppermute x6 -> x0, starting transfers between devices: 21.3 us -> none  [the longest x4 10.4 us: passed_along(): lax.ppermute(array, axis, [(i, (i + by) % devices) for i in range(devices)])]
    ppermute x6 -> x0, waiting for transfers between devices: 19.8 us -> none  [the longest x4 19.8 us: passed_along(): lax.ppermute(array, axis, [(i, (i + by) % devices) for i in range(devices)])]
    add x1 -> x0, other arithmetic: 10.1 us -> none  [lookup_stiffness(): summed + jnp.where(material == level, stiffness[level], jnp.float32(0.0))]
    select_n x4 -> x0, other arithmetic: 8.29 us -> none  [the longest x2 8.28 us: shards(): jnp.take(flat_image, send_rows[0, offset], axis=1)]
    mul x11 -> x0, other arithmetic: 6.1 us -> none  [the longest x2 3.52 us: shards(): masked = eigen_basis[0] * column_mask[:, None, None, None, None]]
  transfers between devices with their start and end apart: 6 -> 0, of which waited for: 3 -> 0; matrix products, arithmetic and copies ran while one was open for 19% -> 0% of each run, Pallas kernels for 0% -> 0%
where the time goes in v1:
time: 120 us
  Pallas kernels  112 us (93%)
  local copies, waits for them, and re-layouts  6.56 us (5%)
  between operations  1.3 us (1%)
    pallas_call x1, Pallas kernels, shards(): pl.pallas_call(kernel, out_shape=(jax.ShapeDtypeStruct((1, K, K), F32), j...  112 us
    unnamed x14, local copies, waits for them, and re-layouts  6.56 us

profile of v1, /device:TPU:1, one launch (start us, length us, event | category | flops | bytes accessed | tf_op | source)
XLA Modules:
  0.0 119.5 jit_solution(12266047041823120307)
XLA Ops:
  1.3 0.0 copy-start
  1.3 1.3 %copy-done = bf16[1,48,3,2,16,128]{5,4,3,2,1,0:T(8,128)(2,1)S(1)} copy-done((bf16[1,48,3,2,16,128]{5,4,3,2,1,0:T(8,128)(2,1)S(1)}, bf16[1,48,3,2,16,128]{5,4,3,2,1,0:T(8,128)(2,1)}, u32[]{:S(2)}) %copy-start) | copy-done | bytes 1179672
  2.5 0.0 copy-start.1
  2.6 1.2 %copy-done.1 = s32[1,128,16,128]{3,2,1,0:T(8,128)S(1)} copy-done((s32[1,128,16,128]{3,2,1,0:T(8,128)S(1)}, s32[1,128,16,128]{3,2,1,0:T(8,128)}, u32[]{:S(2)}) %copy-start.1) | copy-done | bytes 1048600
  3.8 0.0 copy-start.2
  3.8 0.8 copy-done.2
  4.5 0.0 copy-start.3
  4.5 0.8 copy-done.3
  5.3 0.0 copy-start.4
  5.3 0.7 copy-done.4
  5.9 0.0 copy-start.5
  5.9 0.7 copy-done.5
  6.6 111.7 %coarse.1 = (f32[1,48,48]{2,1,0:T(8,128)S(1)}, f32[1,4,48,48]{3,2,1,0:T(8,128)S(1)}) custom-call(s32[1]{0:T(128)S(6)} %copy.11.counts, s32[1,2]{1,0:T(1,128)S(1)} %copy-done.4, f32[16]{0:T(128)S(1)} %copy-done.5, bf16[1,48,3,2,16,128]{5,4,3,2,1,0:T(8,128)(2,1)S(1)} %copy-done, s32[1,128,16,128]{3,2,1,0:T(8,128)S(1)} %copy-done.1, ...), custom_call_target="tpu_custom_call" | custom-call | tf_op jit(solution)/shard_map/coarse/pallas_call | solution.py:367
  118.3 0.6 copy.12
  118.9 0.6 copy.13
Async XLA Ops:
  1.3 1.3 %copy-start = (bf16[1,48,3,2,16,128]{5,4,3,2,1,0:T(8,128)(2,1)S(1)}, bf16[1,48,3,2,16,128]{5,4,3,2,1,0:T(8,128)(2,1)}, u32[]{:S(2)}) copy-start(bf16[1,48,3,2,16,128]{5,4,3,2,1,0:T(8,128)(2,1)} %eigen.1) | copy-start | bytes 3538948
  2.5 1.2 %copy-start.1 = (s32[1,128,16,128]{3,2,1,0:T(8,128)S(1)}, s32[1,128,16,128]{3,2,1,0:T(8,128)}, u32[]{:S(2)}) copy-start(s32[1,128,16,128]{3,2,1,0:T(8,128)} %material.1) | copy-start | bytes 3145732
  3.8 0.8 copy-start.2
  4.5 0.8 copy-start.3
  5.3 0.7 copy-start.4
  5.9 0.7 copy-start.5

commit v2 on v1

--- a/solution.py
+++ b/solution.py
@@ -29,7 +29,9 @@
 GROUP = 8
 OWNERS = 6
 LANES = 128
-UNROLL = 128
+STRIPS = 8
+STEP = 8
+STRIP = SLAB // STRIPS
 
 
 def at_sub(sub, by):
@@ -68,14 +70,16 @@
     return barrier, sides + 2 + (GROUP - 1) + owner * (7 + 2 * GROUP)
 
 
-def gather(index_of, table, dest, first, count):
+def gather(index, table, dest, first, count):
     def body(step, carry):
-        base = pl.multiple_of(step * UNROLL, UNROLL)
-        for u in range(UNROLL):
-            dest[pl.ds(base + u, 1), :] = table[pl.ds(index_of(first + base + u), 1), :]
+        base = pl.multiple_of(step * (STRIPS * STEP), STRIPS * STEP)
+        at = first // STRIPS + step * STEP
+        for q in range(STRIPS):
+            for j in range(STEP):
+                dest[pl.ds(base + (q * STEP + j), 1), :] = table[pl.ds(index[q][at + j], 1), :]
         return carry
 
-    lax.fori_loop(0, count // UNROLL, body, 0)
+    lax.fori_loop(0, count // (STRIPS * STEP), body, 0)
 
 
 def widen(tile):
@@ -83,39 +87,47 @@
 
 
 def kernel(
-    counts, couple, stiffness, eigen, material, own_rows, send_rows,
+    counts_in, couple_in, stiffness_in, eigen, material, own_rows, send_rows,
     diag_out, off_out,
-    eig, halo, mat, coef, field, image, table, own_sel, send_sel, packed, arrived,
-    own_index, send_index, part, sums, zsums, piece, whole, forward,
+    counts, couple, stiffness, eig, halo, mat, coef, field, image, table, own_sel, send_sel, packed, arrived,
+    part, sums, zsums, piece, whole, forward,
     load_sem, halo_send, halo_recv, slab_send, slab_recv,
-    one_send, one_recv, two_send, two_recv, three_send, three_recv, fwd_send, fwd_recv,
+    one_send, one_recv, two_send, two_recv, three_send, three_recv, fwd_send, fwd_recv, index_sem, *strips,
 ):
     sub, row = lax.axis_index("sub"), lax.axis_index("row")
     z, place = row // GROUP, lax.rem(row, GROUP)
     barrier, greetings = start_barrier(sub, row)
 
     loads = [pltpu.make_async_copy(eigen.at[0], eig, load_sem.at[0])]
-    loads.append(pltpu.make_async_copy(own_rows, own_index, load_sem.at[1]))
-    loads.append(pltpu.make_async_copy(send_rows, send_index, load_sem.at[2]))
+    own_index = [strips[o * STRIPS : (o + 1) * STRIPS] for o in (0, 1)]
+    send_index = [strips[(2 + o) * STRIPS : (3 + o) * STRIPS] for o in (0, 1)]
+    index_loads = []
+    for kind, (rows, index) in enumerate(((own_rows, own_index), (send_rows, send_index))):
+        index_loads.append([])
+        for o in (1, 0):
+            for q in range(STRIPS):
+                index_loads[kind].append(pltpu.make_async_copy(
+                    rows.at[0, o, pl.ds(q * STRIP, STRIP)], index[o][q], index_sem.at[kind, o, q]))
     for p in range(CX + 2):
         plane = jnp.clip(row * CX + (p - 1), 0, PLANES - 1)
-        loads.append(pltpu.make_async_copy(material.at[0, plane], mat.at[p], load_sem.at[3 + p]))
-    for load in loads:
+        loads.append(pltpu.make_async_copy(material.at[0, plane], mat.at[p], load_sem.at[1 + p]))
+    loads.append(pltpu.make_async_copy(counts_in, counts, load_sem.at[3 + CX]))
+    loads.append(pltpu.make_async_copy(couple_in, couple, load_sem.at[4 + CX]))
+    loads.append(pltpu.make_async_copy(stiffness_in, stiffness, load_sem.at[5 + CX]))
+    for load in loads + index_loads[0] + index_loads[1]:
         load.start()
-
+    loads[3 + CX].wait()
     count = counts[0]
 
     def kept(k):
         return (k < count).astype(F32)
 
-    loads[0].wait()
-
     pl.semaphore_wait(barrier, greetings)
     up = pltpu.make_async_remote_copy(
-        src_ref=eig.at[:, :, CX - 1], dst_ref=halo.at[0], send_sem=halo_send.at[0],
+        src_ref=eigen.at[0, :, :, CX - 1], dst_ref=halo.at[0], send_sem=halo_send.at[0],
         recv_sem=halo_recv.at[0], device_id=(sub, jnp.minimum(row + 1, NROW - 1)), device_id_type=MESH)
     down = pltpu.make_async_remote_copy(
-        src_ref=eig.at[:, :, 0], dst_ref=halo.at[1], send_sem=halo_send.at[1],
+        src_ref=eigen.at[0, :, :, 0], dst_ref=halo.at[1], send_sem=halo_send.at[1],
         recv_sem=halo_recv.at[1], device_id=(sub, jnp.maximum(row - 1, 0)), device_id_type=MESH)
 
     @pl.when(row < NROW - 1)
@@ -133,6 +145,8 @@
     @pl.when(row == NROW - 1)
     def _():
         halo[1] = jnp.zeros((K, C, GY, GZ), BF16)
+
+    loads[0].wait()
 
     def mask_column(k, carry):
         keep = kept(k)
@@ -147,29 +161,29 @@
     def across(source, at):
         return source[pl.ds(at, K, stride=C * CX * GY), :]
 
-    def fill_table(at, carry):
-        table[pl.ds(pl.multiple_of(at * GZ, GZ), GZ), :] = widen(across(field, at).T)
+    def fill_table(block, carry):
+        for y in range(GY):
+            at = block * GY + y
+            table[pl.ds(pl.multiple_of(at * GZ, GZ), GZ), :] = widen(across(field, at).T)
         return carry
 
-    lax.fori_loop(0, C * CX * GY, fill_table, 0)
-
-    loads[1].wait()
+    lax.fori_loop(0, C * CX, fill_table, 0)
+
+    for load in index_loads[0]:
+        load.wait()
+    loads[4 + CX].wait()
     lane = lax.broadcasted_iota(jnp.int32, (K, LANES), 1)
     line = lax.broadcasted_iota(jnp.int32, (K, LANES), 0)
     slabs = []
     for o in (1, 0):
         turn = jnp.where(lane == line, couple[0, o].astype(F32), F32(0)).astype(BF16)
         for n in range(NCHUNK):
-            gather(lambda t: own_index[0, o, t], table, own_sel, n * CHUNK, CHUNK)
-
-            def turned(step, carry):
-                base = pl.multiple_of(step * 256, 256)
+            gather(own_index[o], table, own_sel, n * CHUNK, CHUNK)
+
+            for base in range(0, CHUNK, 256):
                 picked = own_sel[pl.ds(base, 256), :].astype(BF16)
                 packed[o, n, :, pl.ds(base, 256)] = lax.dot_general(
                     turn, picked, (((1,), (1,)), ((), ())), preferred_element_type=F32).astype(BF16)
-                return carry
-
-            lax.fori_loop(0, CHUNK // 256, turned, 0)
             slab = pltpu.make_async_remote_copy(
                 src_ref=packed.at[o, n], dst_ref=arrived.at[o, n],
                 send_sem=slab_send.at[o, n], recv_sem=slab_recv.at[o, n],
@@ -178,7 +192,8 @@
             slabs.append(slab)
 
     for p in range(CX + 2):
-        loads[3 + p].wait()
+        loads[1 + p].wait()
+    loads[5 + CX].wait()
     kappa = []
     for p in range(CX + 2):
         level = mat[p]
@@ -186,6 +201,7 @@
         for m in range(NLEVEL):
             found = found + jnp.where(level == m, stiffness[m], F32(0))
         kappa.append(found)
+    faces = []
     for p in range(CX + 1):
         face = 0.5 * (kappa[p] + kappa[p + 1])
         if p == 0:
@@ -193,12 +209,19 @@
         if p == CX:
             face = face * (row < NROW - 1).astype(F32)
         coef[p] = face
+        faces.append(face)
     in_y = lax.broadcasted_iota(jnp.int32, (GY, GZ), 0) < GY - 1
     in_z = lax.broadcasted_iota(jnp.int32, (GY, GZ), 1) < GZ - 1
     for p in range(CX):
         mid = kappa[p + 1]
-        coef[CX + 1 + p] = jnp.where(in_y, 0.5 * (mid + pltpu.roll(mid, GY - 1, 0)), 0.0)
-        coef[2 * CX + 1 + p] = jnp.where(in_z, 0.5 * (mid + pltpu.roll(mid, GZ - 1, 1)), 0.0)
+        y_up = jnp.where(in_y, 0.5 * (mid + pltpu.roll(mid, GY - 1, 0)), 0.0)
+        z_up = jnp.where(in_z, 0.5 * (mid + pltpu.roll(mid, GZ - 1, 1)), 0.0)
+        y_down, z_down = pltpu.roll(y_up, 1, 0), pltpu.roll(z_up, 1, 1)
+        for n, face in enumerate((y_down, y_up, z_down, z_up)):
+            coef[CX + 1 + 4 * p + n] = face
+        along = (faces[p] + faces[p + 1], y_down + y_up, z_down + z_up)
+        for c in range(C):
+            coef[5 * CX + 1 + C * p + c] = along[0] + along[1] + along[2] + 2.0 * along[c]
 
     @pl.when(row > 0)
     def _():
@@ -208,7 +231,7 @@
     def _():
         down.wait_recv()
 
-    def apply_column(k, carry):
+    def apply_column(k):
         keep = kept(k)
         for c in range(C):
             def at(p):
@@ -217,33 +240,41 @@
             cells = [halo[0, k, c].astype(F32) * keep]
             cells += [field[pl.ds(at(p), GY), :] for p in range(CX)]
             cells.append(halo[1, k, c].astype(F32) * keep)
-            flux = [coef[p] * (cells[p + 1] - cells[p]) for p in range(CX + 1)]
             for p in range(CX):
                 u = cells[p + 1]
-                term_x = flux[p] - flux[p + 1]
-                flux_y = coef[CX + 1 + p] * (pltpu.roll(u, GY - 1, 0) - u)
-                term_y = pltpu.roll(flux_y, 1, 0) - flux_y
-                flux_z = coef[2 * CX + 1 + p] * (pltpu.roll(u, GZ - 1, 1) - u)
-                term_z = pltpu.roll(flux_z, 1, 1) - flux_z
-                terms = [term_x, term_y, term_z]
-                terms[c] = 3.0 * terms[c]
-                total = terms[0] + terms[1] + terms[2]
-                image[pl.ds(at(p), GY), :] = total.astype(BF16).astype(F32)
+                face = [coef[CX + 1 + 4 * p + n] for n in range(4)]
+                near = [
+                    coef[p] * cells[p] + coef[p + 1] * cells[p + 2],
+                    face[0] * pltpu.roll(u, 1, 0) + face[1] * pltpu.roll(u, GY - 1, 0),
+                    face[2] * pltpu.roll(u, 1, 1) + face[3] * pltpu.roll(u, GZ - 1, 1),
+                ]
+                own = coef[5 * CX + 1 + C * p + c]
+                image[pl.ds(at(p), GY), :] = own * u - (near[0] + near[1] + near[2] + 2.0 * near[c])
+
+    def apply_columns(block, carry):
+        for u in range(4):
+            apply_column(4 * block + u)
         return carry
 
-    lax.fori_loop(0, K, apply_column, 0)
-
-    def image_table(at, total):
-        turned = widen(across(image, at).T)
-        table[pl.ds(pl.multiple_of(at * GZ, GZ), GZ), :] = turned
+    lax.fori_loop(0, K // 4, apply_columns, 0)
+
+    def image_table(block, total):
+        basis, turned = [], []
+        for y in range(GY):
+            at = block * GY + y
+            wide = widen(across(image, at).T)
+            table[pl.ds(pl.multiple_of(at * GZ, GZ), GZ), :] = wide
+            turned.append(wide.astype(BF16))
+            basis.append(across(field, at).astype(BF16))
         return total + jnp.dot(
-            across(field, at).astype(BF16), turned.astype(BF16), preferred_element_type=F32)
-
-    diag = lax.fori_loop(0, C * CX * GY, image_table, jnp.zeros((K, LANES), F32))
-
-    loads[2].wait()
+            jnp.concatenate(basis, axis=1), jnp.concatenate(turned, axis=0), preferred_element_type=F32)
+
+    diag = lax.fori_loop(0, C * CX, image_table, jnp.zeros((K, LANES), F32))
+
+    for load in index_loads[1]:
+        load.wait()
     for o in (1, 0):
-        gather(lambda t: send_index[0, o, t], table, send_sel.at[o], 0, SLAB)
+        gather(send_index[o], table, send_sel.at[o], 0, SLAB)
 
     mats = [diag]
     for o in (0, 1):
@@ -360,20 +391,22 @@
 
 
 def shards(eigen_basis, material, counts, couple, own_rows, send_rows, stiffness):
-    smem = pl.BlockSpec(memory_space=pltpu.SMEM)
-    anywhere = pl.BlockSpec(memory_space=pl.ANY)
+    hbm = pl.BlockSpec(memory_space=pltpu.HBM)
     vmem = pl.BlockSpec(memory_space=pltpu.VMEM)
     dma = pltpu.SemaphoreType.DMA
     return pl.pallas_call(
         kernel,
         out_shape=(jax.ShapeDtypeStruct((1, K, K), F32), jax.ShapeDtypeStruct((1, 4, K, K), F32)),
-        in_specs=[smem, smem, smem, anywhere, anywhere, anywhere, anywhere],
+        in_specs=[hbm] * 7,
         out_specs=(vmem, vmem),
         scratch_shapes=[
+            pltpu.SMEM((1,), jnp.int32),
+            pltpu.SMEM((1, 2), jnp.int32),
+            pltpu.SMEM((NLEVEL,), F32),
             pltpu.VMEM((K, C, CX, GY, GZ), BF16),
             pltpu.VMEM((2, K, C, GY, GZ), BF16),
             pltpu.VMEM((CX + 2, GY, GZ), jnp.int32),
-            pltpu.VMEM((3 * CX + 1, GY, GZ), F32),
+            pltpu.VMEM((5 * CX + 1 + C * CX, GY, GZ), F32),
             pltpu.VMEM((K * C * CX * GY, GZ), F32),
             pltpu.VMEM((K * C * CX * GY, GZ), F32),
             pltpu.VMEM((ROWS, LANES), F32),
@@ -381,20 +414,19 @@
             pltpu.VMEM((2, SLAB, LANES), F32),
             pltpu.VMEM((2, NCHUNK, K, CHUNK), BF16),
             pltpu.VMEM((2, NCHUNK, K, CHUNK), BF16),
-            pltpu.SMEM((1, 2, SLAB), jnp.int32),
-            pltpu.SMEM((1, 2, SLAB), jnp.int32),
             pltpu.VMEM((OWNERS, 24, LANES), F32),
             pltpu.VMEM((GROUP, 24, LANES), F32),
             pltpu.VMEM((8, 24, LANES), F32),
             pltpu.VMEM((2, 24, LANES), F32),
             pltpu.VMEM((OWNERS, 24, LANES), F32),
             pltpu.VMEM((2, OWNERS, 8, LANES), F32),
-            dma((3 + CX + 2,)), dma((2,)), dma((2,)), dma((2, NCHUNK)), dma((2, NCHUNK)),
+            dma((6 + CX,)), dma((2,)), dma((2,)), dma((2, NCHUNK)), dma((2, NCHUNK)),
             dma((GROUP,)), dma((GROUP,)), dma((8,)), dma((8,)),
             dma((GROUP,)), dma((OWNERS,)), dma((2, GROUP)), dma((2, OWNERS)),
-        ],
+            dma((2, 2, STRIPS)),
+        ] + [pltpu.SMEM((STRIP,), jnp.int32) for _ in range(4 * STRIPS)],
         compiler_params=pltpu.CompilerParams(
-            collective_id=0, has_side_effects=True, vmem_limit_bytes=48 * 2**20),
+            collective_id=0, has_side_effects=True, vmem_limit_bytes=60 * 2**20),
         name="coarse",
     )(counts, couple, stiffness, eigen_basis, material, own_rows, send_rows)
 

time: 120 us -> 67.4 us (0.56)
  Pallas kernels: 112 us -> 63 us
  local copies, waits for them, and re-layouts: 6.56 us -> 2.89 us
    pallas_call x1, Pallas kernels: 112 us -> 63 us  [shards(): pl.pallas_call(kernel, out_shape=(jax.ShapeDtypeStruct((1, K, K), F32), j...]
    unnamed x14 -> x2, local copies, waits for them, and re-layouts: 6.56 us -> 2.89 us
where the time goes in v2:
time: 67.4 us; the launch traced here: 67.2 us
  Pallas kernels  63 us (93%)
  local copies, waits for them, and re-layouts  2.89 us (4%)
  between operations  1.29 us (2%)
    pallas_call x1, Pallas kernels, shards(): pl.pallas_call(kernel, out_shape=(jax.ShapeDtypeStruct((1, K, K), F32), j...  63 us
    unnamed x2, local copies, waits for them, and re-layouts  2.89 us

profile of v2, /device:TPU:1, one launch (start us, length us, event | category | flops | bytes accessed | tf_op | source)
XLA Modules:
  0.0 67.2 jit_solution(12673605783334014867)
XLA Ops:
  1.3 63.0 %coarse.1 = (f32[1,48,48]{2,1,0:T(8,128)}, f32[1,4,48,48]{3,2,1,0:T(8,128)}) custom-call(s32[1]{0:T(128)S(6)} %copy.11.counts_in, s32[1,2]{1,0:T(1,128)} %couple_in.1, f32[16]{0:T(128)} %stiffness_in.1, bf16[1,48,3,2,16,128]{5,4,3,2,1,0:T(8,128)(2,1)} %eigen.1, s32[1,128,16,128]{3,2,1,0:T(8,128)} %material.1, s32[1,2,4096]{2,1,0:T(2,128)} %own_rows.1, ...), custom_call_target="tpu_custom_call" | custom-call | tf_op jit(solution)/shard_map/coarse/pallas_call | solution.py:397
  64.3 1.3 %copy.12 = f32[1,48,48]{2,1,0:T(8,128)} copy(f32[1,48,48]{2,1,0:T(8,128)} %get-tuple-element.4) | data formatting | bytes 18432
  65.6 1.5 %copy.13 = f32[1,4,48,48]{3,2,1,0:T(8,128)} copy(f32[1,4,48,48]{3,2,1,0:T(8,128)} %get-tuple-element.5) | data formatting | bytes 73728

commit v3 on v2

--- a/solution.py
+++ b/solution.py
@@ -23,8 +23,12 @@
 NROW = 64
 PLANES = NROW * CX
 SLAB = 4096
-CHUNK = 1024
+CHUNK = 512
 NCHUNK = SLAB // CHUNK
+BACK = 3
+UP = [(1, n) for n in range(NCHUNK - BACK)] + [(0, n) for n in range(NCHUNK)]
+DOWN = [(1, n) for n in range(NCHUNK - BACK, NCHUNK)]
+FAR_FIRST = (4, 3, 5, 2, 6, 1, 7)
 NLEVEL = 16
 GROUP = 8
 OWNERS = 6
@@ -53,21 +57,23 @@
     def _():
         signal(sub, row + 1)
 
-    for by in (1, 2):
-        signal(at_sub(sub, -by), row)
+    for by in (-1, -2, 2):
+        signal(at_sub(sub, by), row)
+    for step in FAR_FIRST:
+        signal(sub, z * GROUP + lax.rem(place + step, GROUP))
+
+    @pl.when(place < OWNERS)
+    def _():
+        for step in FAR_FIRST:
+            signal(sub, lax.rem(z + step, 8) * GROUP + place)
+
+    for by in (2, -2, 1):
         for q in range(OWNERS):
             signal(at_sub(sub, by), z * GROUP + q)
-    for step in range(1, GROUP):
-        signal(sub, z * GROUP + lax.rem(place + step, GROUP))
-
-    @pl.when(place < OWNERS)
-    def _():
-        for step in range(1, 8):
-            signal(sub, lax.rem(z + step, 8) * GROUP + place)
 
     owner = (place < OWNERS).astype(jnp.int32)
     sides = (row > 0).astype(jnp.int32) + (row < NROW - 1).astype(jnp.int32)
-    return barrier, sides + 2 + (GROUP - 1) + owner * (7 + 2 * GROUP)
+    return barrier, sides + 3 + (GROUP - 1) + owner * (7 + 3 * GROUP)
 
 
 def gather(index, table, dest, first, count):
@@ -89,9 +95,9 @@
 def kernel(
     counts_in, couple_in, stiffness_in, eigen, material, own_rows, send_rows,
     diag_out, off_out,
-    counts, couple, stiffness, eig, halo, mat, coef, field, image, table, own_sel, send_sel, packed, arrived,
+    counts, couple, stiffness, eig, halo, mat, coef, field, image, table, own_sel, own_kept, send_sel, packed, arrived, down_packed, down_arrived,
     part, sums, zsums, piece, whole, forward,
-    load_sem, halo_send, halo_recv, slab_send, slab_recv,
+    load_sem, halo_send, halo_recv, slab_send, slab_recv, down_send, down_recv,
     one_send, one_recv, two_send, two_recv, three_send, three_recv, fwd_send, fwd_recv, index_sem, *strips,
 ):
     sub, row = lax.axis_index("sub"), lax.axis_index("row")
@@ -122,6 +128,37 @@
     def kept(k):
         return (k < count).astype(F32)
 
+    @pl.when(row == 0)
+    def _():
+        halo[0] = jnp.zeros((K, C, GY, GZ), BF16)
+
+    @pl.when(row == NROW - 1)
+    def _():
+        halo[1] = jnp.zeros((K, C, GY, GZ), BF16)
+
+    loads[0].wait()
+
+    def mask_column(k, carry):
+        keep = kept(k)
+        for c in range(C):
+            for p in range(CX):
+                base = pl.multiple_of(k * (C * CX * GY) + (c * CX + p) * GY, GY)
+                field[pl.ds(base, GY), :] = eig[k, c, p].astype(F32) * keep
+        return carry
+
+    lax.fori_loop(0, K, mask_column, 0)
+
+    def across(source, at):
+        return source[pl.ds(at, K, stride=C * CX * GY), :]
+
+    def fill_table(block, carry):
+        for y in range(GY):
+            at = block * GY + y
+            table[pl.ds(pl.multiple_of(at * GZ, GZ), GZ), :] = widen(across(field, at).T)
+        return carry
+
+    lax.fori_loop(0, C * CX, fill_table, 0)
+
     pl.semaphore_wait(barrier, greetings)
     up = pltpu.make_async_remote_copy(
         src_ref=eigen.at[0, :, :, CX - 1], dst_ref=halo.at[0], send_sem=halo_send.at[0],
@@ -138,58 +175,33 @@
     def _():
         down.start()
 
-    @pl.when(row == 0)
-    def _():
-        halo[0] = jnp.zeros((K, C, GY, GZ), BF16)
-
-    @pl.when(row == NROW - 1)
-    def _():
-        halo[1] = jnp.zeros((K, C, GY, GZ), BF16)
-
-    loads[0].wait()
-
-    def mask_column(k, carry):
-        keep = kept(k)
-        for c in range(C):
-            for p in range(CX):
-                base = pl.multiple_of(k * (C * CX * GY) + (c * CX + p) * GY, GY)
-                field[pl.ds(base, GY), :] = eig[k, c, p].astype(F32) * keep
-        return carry
-
-    lax.fori_loop(0, K, mask_column, 0)
-
-    def across(source, at):
-        return source[pl.ds(at, K, stride=C * CX * GY), :]
-
-    def fill_table(block, carry):
-        for y in range(GY):
-            at = block * GY + y
-            table[pl.ds(pl.multiple_of(at * GZ, GZ), GZ), :] = widen(across(field, at).T)
-        return carry
-
-    lax.fori_loop(0, C * CX, fill_table, 0)
-
     for load in index_loads[0]:
         load.wait()
     loads[4 + CX].wait()
     lane = lax.broadcasted_iota(jnp.int32, (K, LANES), 1)
     line = lax.broadcasted_iota(jnp.int32, (K, LANES), 0)
+    turn = [
+        jnp.where(lane == line, couple[0, o].astype(F32), F32(0)).astype(BF16) for o in (0, 1)]
+    plain = jnp.where(lane == line, F32(1), F32(0)).astype(BF16)
+
+    def turned(by, rows):
+        return jnp.concatenate([
+            lax.dot_general(by, rows[base : base + 256].astype(BF16), (((1,), (1,)), ((), ())),
+                            preferred_element_type=F32).astype(BF16)
+            for base in range(0, CHUNK, 256)], axis=1)
+
     slabs = []
-    for o in (1, 0):
-        turn = jnp.where(lane == line, couple[0, o].astype(F32), F32(0)).astype(BF16)
-        for n in range(NCHUNK):
-            gather(own_index[o], table, own_sel, n * CHUNK, CHUNK)
-
-            for base in range(0, CHUNK, 256):
-                picked = own_sel[pl.ds(base, 256), :].astype(BF16)
-                packed[o, n, :, pl.ds(base, 256)] = lax.dot_general(
-                    turn, picked, (((1,), (1,)), ((), ())), preferred_element_type=F32).astype(BF16)
-            slab = pltpu.make_async_remote_copy(
-                src_ref=packed.at[o, n], dst_ref=arrived.at[o, n],
-                send_sem=slab_send.at[o, n], recv_sem=slab_recv.at[o, n],
-                device_id=(at_sub(sub, o + 1), row), device_id_type=MESH)
-            slab.start()
-            slabs.append(slab)
+    for e, (o, n) in enumerate(UP):
+        gather(own_index[o], table, own_sel.at[e % 2], n * CHUNK, CHUNK)
+        packed[e] = turned(turn[o], own_sel[e % 2])
+        slab = pltpu.make_async_remote_copy(
+            src_ref=packed.at[e], dst_ref=arrived.at[e],
+            send_sem=slab_send.at[e], recv_sem=slab_recv.at[e],
+            device_id=(at_sub(sub, o + 1), row), device_id_type=MESH)
+        slab.start()
+        slabs.append(slab)
+    for e, (o, n) in enumerate(DOWN):
+        gather(own_index[o], table, own_kept.at[e], n * CHUNK, CHUNK)
 
     for p in range(CX + 2):
         loads[1 + p].wait()
@@ -273,32 +285,45 @@
 
     for load in index_loads[1]:
         load.wait()
-    for o in (1, 0):
-        gather(send_index[o], table, send_sel.at[o], 0, SLAB)
-
-    mats = [diag]
-    for o in (0, 1):
-        for n in range(NCHUNK):
-            slabs[(1 - o) * NCHUNK + n].wait_recv()
-
-        def multiply(step, total, o=o):
-            n = step
-            picked = send_sel[o, pl.ds(pl.multiple_of(n * CHUNK, CHUNK), CHUNK), :].astype(BF16)
-            return total + jnp.dot(arrived[o, n], picked, preferred_element_type=F32)
-
-        mats.append(lax.fori_loop(0, NCHUNK, multiply, jnp.zeros((K, LANES), F32)))
+    downs = []
+    for e, (o, n) in enumerate(DOWN):
+        gather(send_index[o], table, own_sel.at[e % 2], n * CHUNK, CHUNK)
+        down_packed[e] = turned(plain, own_sel[e % 2])
+        slab = pltpu.make_async_remote_copy(
+            src_ref=down_packed.at[e], dst_ref=down_arrived.at[e],
+            send_sem=down_send.at[e], recv_sem=down_recv.at[e],
+            device_id=(at_sub(sub, -o - 1), row), device_id_type=MESH)
+        slab.start()
+        downs.append(slab)
+    pairs = [jnp.zeros((K, LANES), F32) for o in (0, 1)]
+    for e, (o, n) in enumerate(UP):
+        gather(send_index[o], table, send_sel.at[e % 2], n * CHUNK, CHUNK)
+        slabs[e].wait_recv()
+        pairs[o] = pairs[o] + jnp.dot(
+            arrived[e], send_sel[e % 2].astype(BF16), preferred_element_type=F32)
+    below = jnp.zeros((K, LANES), F32)
+    for e, (o, n) in enumerate(DOWN):
+        downs[e].wait_recv()
+        below = below + jnp.dot(
+            down_arrived[e], own_kept[e].astype(BF16), preferred_element_type=F32)
+    mats = [diag, pairs[0], pairs[1], below * couple[0, 1].astype(F32)]
     for q in range(OWNERS):
-        for m in range(3):
+        for m in range(4):
             part[q, pl.ds(8 * m, 8), :] = mats[m][8 * q : 8 * q + 8]
 
     is_owner = place < OWNERS
+    own_q = jnp.minimum(place, OWNERS - 1)
+
+    def landed(ref, sem):
+        pltpu.make_async_copy(ref, ref, sem).wait()
+
     firsts = []
-    for step in range(1, GROUP):
+    for step in FAR_FIRST:
         to = lax.rem(place + step, GROUP)
         to_q = jnp.minimum(to, OWNERS - 1)
         firsts.append((to, pltpu.make_async_remote_copy(
             src_ref=part.at[to_q], dst_ref=sums.at[place],
-            send_sem=one_send.at[step], recv_sem=one_recv.at[place],
+            send_sem=one_send.at[step], recv_sem=one_recv,
             device_id=(sub, z * GROUP + to), device_id_type=MESH)))
     for to, copy in firsts:
         @pl.when(to < OWNERS)
@@ -306,68 +331,62 @@
             copy.start()
 
     seconds = []
-    for step in range(1, 8):
+    for step in FAR_FIRST:
         seconds.append(pltpu.make_async_remote_copy(
             src_ref=piece.at[0], dst_ref=zsums.at[z],
-            send_sem=two_send.at[step], recv_sem=two_recv.at[z],
+            send_sem=two_send.at[step], recv_sem=two_recv,
             device_id=(sub, lax.rem(z + step, 8) * GROUP + place), device_id_type=MESH))
 
     thirds = []
-    own_q = jnp.minimum(place, OWNERS - 1)
-    for step in range(1, GROUP):
-        thirds.append(pltpu.make_async_remote_copy(
-            src_ref=piece.at[1], dst_ref=whole.at[own_q],
-            send_sem=three_send.at[step], recv_sem=three_recv.at[own_q],
-            device_id=(sub, z * GROUP + lax.rem(place + step, GROUP)), device_id_type=MESH))
-    for o in (0, 1):
+    for o, by in ((1, -2), (2, 2), (0, -1)):
         for to in range(GROUP):
             thirds.append(pltpu.make_async_remote_copy(
                 src_ref=piece.at[1, pl.ds(8 + 8 * o, 8)], dst_ref=forward.at[o, own_q],
-                send_sem=fwd_send.at[o, to], recv_sem=fwd_recv.at[o, own_q],
-                device_id=(at_sub(sub, -o - 1), z * GROUP + to), device_id_type=MESH))
+                send_sem=fwd_send.at[o, to], recv_sem=fwd_recv,
+                device_id=(at_sub(sub, by), z * GROUP + to), device_id_type=MESH))
+    for step in FAR_FIRST:
+        thirds.append(pltpu.make_async_remote_copy(
+            src_ref=piece.at[1], dst_ref=whole.at[own_q],
+            send_sem=three_send.at[step], recv_sem=three_recv,
+            device_id=(sub, z * GROUP + lax.rem(place + step, GROUP)), device_id_type=MESH))
 
     @pl.when(is_owner)
     def _():
-        for step in range(1, GROUP):
-            source = lax.rem(place + step, GROUP)
-            pltpu.make_async_remote_copy(
-                src_ref=part.at[0], dst_ref=sums.at[source], send_sem=one_send.at[step],
-                recv_sem=one_recv.at[source], device_id=(sub, row), device_id_type=MESH).wait_recv()
-        total = part[own_q]
-        for step in range(1, GROUP):
-            total = total + sums[lax.rem(place + step, GROUP)]
+        sums[place] = part[own_q]
+        landed(sums.at[pl.ds(0, GROUP - 1)], one_recv)
+        total = sums[0]
+        for q in range(1, GROUP):
+            total = total + sums[q]
         piece[0] = total
         for copy in seconds:
             copy.start()
-        for step in range(1, 8):
-            source = lax.rem(z + step, 8)
-            pltpu.make_async_remote_copy(
-                src_ref=piece.at[0], dst_ref=zsums.at[source], send_sem=two_send.at[step],
-                recv_sem=two_recv.at[source], device_id=(sub, row), device_id_type=MESH).wait_recv()
-        for step in range(1, 8):
-            total = total + zsums[lax.rem(z + step, 8)]
+        zsums[z] = total
+        landed(zsums.at[pl.ds(0, 7)], two_recv)
+        total = zsums[0]
+        for q in range(1, 8):
+            total = total + zsums[q]
         piece[1] = total
         for copy in thirds:
             copy.start()
         whole[own_q] = total
-
-    for q in range(OWNERS):
-        @pl.when(place != q)
-        def _(q=q):
-            pltpu.make_async_remote_copy(
-                src_ref=piece.at[1], dst_ref=whole.at[q], send_sem=three_send.at[0],
-                recv_sem=three_recv.at[q], device_id=(sub, row), device_id_type=MESH).wait_recv()
-        for o in (0, 1):
-            pltpu.make_async_remote_copy(
-                src_ref=piece.at[1, pl.ds(8, 8)], dst_ref=forward.at[o, q], send_sem=fwd_send.at[o, q],
-                recv_sem=fwd_recv.at[o, q], device_id=(sub, row), device_id_type=MESH).wait_recv()
+        landed(whole.at[pl.ds(0, OWNERS - 1)], three_recv)
+
+    @pl.when(place >= OWNERS)
+    def _():
+        landed(whole, three_recv)
+
+    landed(forward, fwd_recv)
 
     scale = 1.0 / math.sqrt(NROW * SLAB)
     diag_out[0] = jnp.concatenate([whole[q, 0:8, :K] for q in range(OWNERS)], axis=0) * (1.0 / (C * PLANES * GY * GZ))
-    for o in (0, 1):
-        pair = jnp.concatenate([whole[q, 8 + 8 * o : 16 + 8 * o, :] for q in range(OWNERS)], axis=0)
-        off_out[0, 1 - o] = pair.T[:K, :] * scale
-        off_out[0, 2 + o] = jnp.concatenate([forward[o, q, :, :K] for q in range(OWNERS)], axis=0) * scale
+    def joined(ref, at):
+        return jnp.concatenate([ref[q, at : at + 8, :] for q in range(OWNERS)], axis=0)
+
+    from_above = [jnp.concatenate([forward[o, q] for q in range(OWNERS)], axis=0) for o in range(3)]
+    off_out[0, 0] = (joined(whole, 16).T[:K, :] + from_above[2][:, :K]) * scale
+    off_out[0, 1] = joined(whole, 8).T[:K, :] * scale
+    off_out[0, 2] = from_above[0][:, :K] * scale
+    off_out[0, 3] = (from_above[1][:, :K] + joined(whole, 24).T[:K, :]) * scale
 
     @pl.when(row < NROW - 1)
     def _():
@@ -377,7 +396,7 @@
     def _():
         down.wait_send()
 
-    for slab in slabs:
+    for slab in slabs + downs:
         slab.wait_send()
     for to, copy in firsts:
         @pl.when(to < OWNERS)
@@ -410,19 +429,21 @@
             pltpu.VMEM((K * C * CX * GY, GZ), F32),
             pltpu.VMEM((K * C * CX * GY, GZ), F32),
             pltpu.VMEM((ROWS, LANES), F32),
-            pltpu.VMEM((CHUNK, LANES), F32),
-            pltpu.VMEM((2, SLAB, LANES), F32),
-            pltpu.VMEM((2, NCHUNK, K, CHUNK), BF16),
-            pltpu.VMEM((2, NCHUNK, K, CHUNK), BF16),
-            pltpu.VMEM((OWNERS, 24, LANES), F32),
-            pltpu.VMEM((GROUP, 24, LANES), F32),
-            pltpu.VMEM((8, 24, LANES), F32),
-            pltpu.VMEM((2, 24, LANES), F32),
-            pltpu.VMEM((OWNERS, 24, LANES), F32),
-            pltpu.VMEM((2, OWNERS, 8, LANES), F32),
-            dma((6 + CX,)), dma((2,)), dma((2,)), dma((2, NCHUNK)), dma((2, NCHUNK)),
-            dma((GROUP,)), dma((GROUP,)), dma((8,)), dma((8,)),
-            dma((GROUP,)), dma((OWNERS,)), dma((2, GROUP)), dma((2, OWNERS)),
+            pltpu.VMEM((2, CHUNK, LANES), F32),
+            pltpu.VMEM((BACK, CHUNK, LANES), F32),
+            pltpu.VMEM((2, CHUNK, LANES), F32),
+            pltpu.VMEM((len(UP), K, CHUNK), BF16),
+            pltpu.VMEM((len(UP), K, CHUNK), BF16),
+            pltpu.VMEM((BACK, K, CHUNK), BF16),
+            pltpu.VMEM((BACK, K, CHUNK), BF16),
+            pltpu.VMEM((OWNERS, 32, LANES), F32),
+            pltpu.VMEM((GROUP, 32, LANES), F32),
+            pltpu.VMEM((8, 32, LANES), F32),
+            pltpu.VMEM((2, 32, LANES), F32),
+            pltpu.VMEM((OWNERS, 32, LANES), F32),
+            pltpu.VMEM((3, OWNERS, 8, LANES), F32),
+            dma((6 + CX,)), dma((2,)), dma((2,)), dma((len(UP),)), dma((len(UP),)), dma((BACK,)), dma((BACK,)),
+            dma((GROUP,)), dma, dma((8,)), dma, dma((GROUP,)), dma, dma((3, GROUP)), dma,
             dma((2, 2, STRIPS)),
         ] + [pltpu.SMEM((STRIP,), jnp.int32) for _ in range(4 * STRIPS)],
         compiler_params=pltpu.CompilerParams(

time: 67.4 us -> 61.6 us (0.914)
  Pallas kernels: 63 us -> 57.2 us
    pallas_call x1, Pallas kernels: 63 us -> 57.2 us  [shards(): pl.pallas_call(kernel, out_shape=(jax.ShapeDtypeStruct((1, K, K), F32), j...]
where the time goes in v3:
time: 61.6 us; the launch traced here: 61.4 us
  Pallas kernels  57.2 us (93%)
  local copies, waits for them, and re-layouts  2.89 us (5%)
  between operations  1.29 us (2%)
    pallas_call x1, Pallas kernels, shards(): pl.pallas_call(kernel, out_shape=(jax.ShapeDtypeStruct((1, K, K), F32), j...  57.2 us
    unnamed x2, local copies, waits for them, and re-layouts  2.89 us

profile of v3, /device:TPU:1, one launch (start us, length us, event | category | flops | bytes accessed | tf_op | source)
XLA Modules:
  0.0 61.4 jit_solution(9568188247670826837)
XLA Ops:
  1.3 57.2 %coarse.1 = (f32[1,48,48]{2,1,0:T(8,128)}, f32[1,4,48,48]{3,2,1,0:T(8,128)}) custom-call(s32[1]{0:T(128)S(6)} %copy.11.counts_in, s32[1,2]{1,0:T(1,128)} %couple_in.1, f32[16]{0:T(128)} %stiffness_in.1, bf16[1,48,3,2,16,128]{5,4,3,2,1,0:T(8,128)(2,1)} %eigen.1, s32[1,128,16,128]{3,2,1,0:T(8,128)} %material.1, s32[1,2,4096]{2,1,0:T(2,128)} %own_rows.1, ...), custom_call_target="tpu_custom_call" | custom-call | tf_op jit(solution)/shard_map/coarse/pallas_call | solution.py:416
  58.5 1.3 %copy.12 = f32[1,48,48]{2,1,0:T(8,128)} copy(f32[1,48,48]{2,1,0:T(8,128)} %get-tuple-element.4) | data formatting | bytes 18432
  59.8 1.5 %copy.13 = f32[1,4,48,48]{3,2,1,0:T(8,128)} copy(f32[1,4,48,48]{3,2,1,0:T(8,128)} %get-tuple-element.5) | data formatting | bytes 73728

commit v4 on v3

--- a/solution.py
+++ b/solution.py
@@ -25,7 +25,7 @@
 SLAB = 4096
 CHUNK = 512
 NCHUNK = SLAB // CHUNK
-BACK = 3
+BACK = 2
 UP = [(1, n) for n in range(NCHUNK - BACK)] + [(0, n) for n in range(NCHUNK)]
 DOWN = [(1, n) for n in range(NCHUNK - BACK, NCHUNK)]
 FAR_FIRST = (4, 3, 5, 2, 6, 1, 7)
@@ -33,9 +33,11 @@
 GROUP = 8
 OWNERS = 6
 LANES = 128
+HALF = 64
 STRIPS = 8
 STEP = 8
 STRIP = SLAB // STRIPS
+PARTS = 2
 
 
 def at_sub(sub, by):
@@ -76,16 +78,17 @@
     return barrier, sides + 3 + (GROUP - 1) + owner * (7 + 3 * GROUP)
 
 
-def gather(index, table, dest, first, count):
+def gather(index, table, dest, first):
     def body(step, carry):
-        base = pl.multiple_of(step * (STRIPS * STEP), STRIPS * STEP)
-        at = first // STRIPS + step * STEP
-        for q in range(STRIPS):
-            for j in range(STEP):
-                dest[pl.ds(base + (q * STEP + j), 1), :] = table[pl.ds(index[q][at + j], 1), :]
+        for part in range(PARTS):
+            start = pl.multiple_of((step * PARTS + part) * (STRIPS * STEP), STRIPS * STEP)
+            at = first // STRIPS + (step * PARTS + part) * STEP
+            for q in range(STRIPS):
+                for j in range(STEP):
+                    dest[pl.ds(start + (q * STEP + j), 1), :] = table[pl.ds(index[q][at + j], 1), :]
         return carry
 
-    lax.fori_loop(0, count // (STRIPS * STEP), body, 0)
+    lax.fori_loop(0, CHUNK // (PARTS * STRIPS * STEP), body, 0)
 
 
 def widen(tile):
@@ -94,7 +97,7 @@
 
 def kernel(
     counts_in, couple_in, stiffness_in, eigen, material, own_rows, send_rows,
-    diag_out, off_out,
+    whole_out, forward_out,
     counts, couple, stiffness, eig, halo, mat, coef, field, image, table, own_sel, own_kept, send_sel, packed, arrived, down_packed, down_arrived,
     part, sums, zsums, piece, whole, forward,
     load_sem, halo_send, halo_recv, slab_send, slab_recv, down_send, down_recv,
@@ -192,7 +195,7 @@
 
     slabs = []
     for e, (o, n) in enumerate(UP):
-        gather(own_index[o], table, own_sel.at[e % 2], n * CHUNK, CHUNK)
+        gather(own_index[o], table, own_sel.at[e % 2], n * CHUNK)
         packed[e] = turned(turn[o], own_sel[e % 2])
         slab = pltpu.make_async_remote_copy(
             src_ref=packed.at[e], dst_ref=arrived.at[e],
@@ -201,7 +204,7 @@
         slab.start()
         slabs.append(slab)
     for e, (o, n) in enumerate(DOWN):
-        gather(own_index[o], table, own_kept.at[e], n * CHUNK, CHUNK)
+        gather(own_index[o], table, own_kept.at[e], n * CHUNK)
 
     for p in range(CX + 2):
         loads[1 + p].wait()
@@ -287,7 +290,7 @@
         load.wait()
     downs = []
     for e, (o, n) in enumerate(DOWN):
-        gather(send_index[o], table, own_sel.at[e % 2], n * CHUNK, CHUNK)
+        gather(send_index[o], table, own_sel.at[e % 2], n * CHUNK)
         down_packed[e] = turned(plain, own_sel[e % 2])
         slab = pltpu.make_async_remote_copy(
             src_ref=down_packed.at[e], dst_ref=down_arrived.at[e],
@@ -297,18 +300,19 @@
         downs.append(slab)
     pairs = [jnp.zeros((K, LANES), F32) for o in (0, 1)]
     for e, (o, n) in enumerate(UP):
-        gather(send_index[o], table, send_sel.at[e % 2], n * CHUNK, CHUNK)
+        gather(send_index[o], table, send_sel.at[e % 2], n * CHUNK)
         slabs[e].wait_recv()
         pairs[o] = pairs[o] + jnp.dot(
             arrived[e], send_sel[e % 2].astype(BF16), preferred_element_type=F32)
     below = jnp.zeros((K, LANES), F32)
-    for e, (o, n) in enumerate(DOWN):
+    for e in range(BACK):
         downs[e].wait_recv()
         below = below + jnp.dot(
             down_arrived[e], own_kept[e].astype(BF16), preferred_element_type=F32)
-    mats = [diag, pairs[0], pairs[1], below * couple[0, 1].astype(F32)]
+    below = below * couple[0, 1].astype(F32)
+    mats = [diag + pltpu.roll(pairs[0], HALF, 1), pairs[1] + pltpu.roll(below, HALF, 1)]
     for q in range(OWNERS):
-        for m in range(4):
+        for m in range(2):
             part[q, pl.ds(8 * m, 8), :] = mats[m][8 * q : 8 * q + 8]
 
     is_owner = place < OWNERS
@@ -334,21 +338,32 @@
     for step in FAR_FIRST:
         seconds.append(pltpu.make_async_remote_copy(
             src_ref=piece.at[0], dst_ref=zsums.at[z],
-            send_sem=two_send.at[step], recv_sem=two_recv,
+            send_sem=two_send, recv_sem=two_recv,
             device_id=(sub, lax.rem(z + step, 8) * GROUP + place), device_id_type=MESH))
 
     thirds = []
     for o, by in ((1, -2), (2, 2), (0, -1)):
         for to in range(GROUP):
             thirds.append(pltpu.make_async_remote_copy(
-                src_ref=piece.at[1, pl.ds(8 + 8 * o, 8)], dst_ref=forward.at[o, own_q],
-                send_sem=fwd_send.at[o, to], recv_sem=fwd_recv,
+                src_ref=piece.at[1, pl.ds(8 if o else 0, 8)], dst_ref=forward.at[o, own_q],
+                send_sem=fwd_send.at[o], recv_sem=fwd_recv,
                 device_id=(at_sub(sub, by), z * GROUP + to), device_id_type=MESH))
     for step in FAR_FIRST:
         thirds.append(pltpu.make_async_remote_copy(
             src_ref=piece.at[1], dst_ref=whole.at[own_q],
-            send_sem=three_send.at[step], recv_sem=three_recv,
+            send_sem=three_send, recv_sem=three_recv,
             device_id=(sub, z * GROUP + lax.rem(place + step, GROUP)), device_id_type=MESH))
+
+    @pl.when(row < NROW - 1)
+    def _():
+        up.wait_send()
+
+    @pl.when(row > 0)
+    def _():
+        down.wait_send()
+
+    for slab in slabs + downs:
+        slab.wait_send()
 
     @pl.when(is_owner)
     def _():
@@ -369,53 +384,52 @@
         for copy in thirds:
             copy.start()
         whole[own_q] = total
+        landed(zsums.at[pl.ds(0, 7)], two_send)
         landed(whole.at[pl.ds(0, OWNERS - 1)], three_recv)
 
-    @pl.when(place >= OWNERS)
-    def _():
-        landed(whole, three_recv)
-
-    landed(forward, fwd_recv)
-
-    scale = 1.0 / math.sqrt(NROW * SLAB)
-    diag_out[0] = jnp.concatenate([whole[q, 0:8, :K] for q in range(OWNERS)], axis=0) * (1.0 / (C * PLANES * GY * GZ))
-    def joined(ref, at):
-        return jnp.concatenate([ref[q, at : at + 8, :] for q in range(OWNERS)], axis=0)
-
-    from_above = [jnp.concatenate([forward[o, q] for q in range(OWNERS)], axis=0) for o in range(3)]
-    off_out[0, 0] = (joined(whole, 16).T[:K, :] + from_above[2][:, :K]) * scale
-    off_out[0, 1] = joined(whole, 8).T[:K, :] * scale
-    off_out[0, 2] = from_above[0][:, :K] * scale
-    off_out[0, 3] = (from_above[1][:, :K] + joined(whole, 24).T[:K, :]) * scale
-
-    @pl.when(row < NROW - 1)
-    def _():
-        up.wait_send()
-
-    @pl.when(row > 0)
-    def _():
-        down.wait_send()
-
-    for slab in slabs + downs:
-        slab.wait_send()
     for to, copy in firsts:
         @pl.when(to < OWNERS)
         def _(copy=copy):
             copy.wait_send()
 
+    @pl.when(place >= OWNERS)
+    def _():
+        landed(whole, three_recv)
+
+    landed(forward, fwd_recv)
+
+    whole_out[...] = whole[...]
+    forward_out[...] = forward[...]
+
     @pl.when(is_owner)
     def _():
-        for copy in seconds + thirds:
-            copy.wait_send()
+        for o in range(3):
+            landed(sums.at[pl.ds(0, GROUP // 2)], fwd_send.at[o])
+        landed(sums.at[pl.ds(0, GROUP - 1)], three_send)
+
+
+def assemble(whole, forward, diag_out, off_out):
+    scale = 1.0 / math.sqrt(NROW * SLAB)
+    diag_pair, pair_below = [
+        jnp.concatenate([whole[q, at : at + 8] for q in range(OWNERS)], axis=0) for at in (0, 8)]
+    from_above = [jnp.concatenate([forward[o, q] for q in range(OWNERS)], axis=0) for o in range(3)]
+    diag_out[0] = diag_pair[:, :K] * (1.0 / (C * PLANES * GY * GZ))
+    off_out[0, 0] = (pair_below.T[:K] + pltpu.roll(from_above[2], HALF, 1)[:, :K]) * scale
+    off_out[0, 1] = diag_pair.T[HALF : HALF + K] * scale
+    off_out[0, 2] = pltpu.roll(from_above[0], HALF, 1)[:, :K] * scale
+    off_out[0, 3] = (from_above[1][:, :K] + pair_below.T[HALF : HALF + K]) * scale
 
 
 def shards(eigen_basis, material, counts, couple, own_rows, send_rows, stiffness):
     hbm = pl.BlockSpec(memory_space=pltpu.HBM)
     vmem = pl.BlockSpec(memory_space=pltpu.VMEM)
     dma = pltpu.SemaphoreType.DMA
-    return pl.pallas_call(
+    sums = pl.pallas_call(
         kernel,
-        out_shape=(jax.ShapeDtypeStruct((1, K, K), F32), jax.ShapeDtypeStruct((1, 4, K, K), F32)),
+        out_shape=(
+            jax.ShapeDtypeStruct((OWNERS, 16, LANES), F32),
+            jax.ShapeDtypeStruct((3, OWNERS, 8, LANES), F32),
+        ),
         in_specs=[hbm] * 7,
         out_specs=(vmem, vmem),
         scratch_shapes=[
@@ -436,20 +450,27 @@
             pltpu.VMEM((len(UP), K, CHUNK), BF16),
             pltpu.VMEM((BACK, K, CHUNK), BF16),
             pltpu.VMEM((BACK, K, CHUNK), BF16),
-            pltpu.VMEM((OWNERS, 32, LANES), F32),
-            pltpu.VMEM((GROUP, 32, LANES), F32),
-            pltpu.VMEM((8, 32, LANES), F32),
-            pltpu.VMEM((2, 32, LANES), F32),
-            pltpu.VMEM((OWNERS, 32, LANES), F32),
+            pltpu.VMEM((OWNERS, 16, LANES), F32),
+            pltpu.VMEM((GROUP, 16, LANES), F32),
+            pltpu.VMEM((8, 16, LANES), F32),
+            pltpu.VMEM((2, 16, LANES), F32),
+            pltpu.VMEM((OWNERS, 16, LANES), F32),
             pltpu.VMEM((3, OWNERS, 8, LANES), F32),
             dma((6 + CX,)), dma((2,)), dma((2,)), dma((len(UP),)), dma((len(UP),)), dma((BACK,)), dma((BACK,)),
-            dma((GROUP,)), dma, dma((8,)), dma, dma((GROUP,)), dma, dma((3, GROUP)), dma,
+            dma((GROUP,)), dma, dma, dma, dma, dma, dma((3,)), dma,
             dma((2, 2, STRIPS)),
         ] + [pltpu.SMEM((STRIP,), jnp.int32) for _ in range(4 * STRIPS)],
         compiler_params=pltpu.CompilerParams(
             collective_id=0, has_side_effects=True, vmem_limit_bytes=60 * 2**20),
         name="coarse",
     )(counts, couple, stiffness, eigen_basis, material, own_rows, send_rows)
+    return pl.pallas_call(
+        assemble,
+        out_shape=(jax.ShapeDtypeStruct((1, K, K), F32), jax.ShapeDtypeStruct((1, 4, K, K), F32)),
+        in_specs=[vmem, vmem],
+        out_specs=(vmem, vmem),
+        name="assemble",
+    )(*sums)
 
 
 def solution(mesh):

time: 61.6 us -> 57.7 us (0.937)
  local copies, waits for them, and re-layouts: 2.89 us -> 0 us
  Pallas kernels: 57.2 us -> 56.3 us
    unnamed x2 -> x0, local copies, waits for them, and re-layouts: 2.89 us -> none
    pallas_call x1 -> x2, Pallas kernels: 57.2 us -> 56.3 us  [the longest x1 54.6 us: shards(): pl.pallas_call(kernel, out_shape=(jax.ShapeDtypeStruct((OWNERS, 16, LANES...]
where the time goes in v4:
time: 57.7 us; the launch traced here: 57.6 us
  Pallas kernels  56.3 us (98%)
  between operations  1.29 us (2%)
    pallas_call x1, Pallas kernels, shards(): pl.pallas_call(kernel, out_shape=(jax.ShapeDtypeStruct((OWNERS, 16, LANES...  54.6 us
    pallas_call x1, Pallas kernels, shards(): pl.pallas_call(assemble, out_shape=(jax.ShapeDtypeStruct((1, K, K), F32),...  1.68 us

profile of v4, /device:TPU:1, one launch (start us, length us, event | category | flops | bytes accessed | tf_op | source)
XLA Modules:
  0.0 57.6 jit_solution(4379150932418206716)
XLA Ops:
  1.3 54.6 %coarse.1 = (f32[6,16,128]{2,1,0:T(8,128)}, f32[3,6,8,128]{3,2,1,0:T(8,128)}) custom-call(s32[1]{0:T(128)S(6)} %copy.9.counts_in, s32[1,2]{1,0:T(1,128)} %couple_in.1, f32[16]{0:T(128)} %stiffness_in.1, bf16[1,48,3,2,16,128]{5,4,3,2,1,0:T(8,128)(2,1)} %eigen.1, s32[1,128,16,128]{3,2,1,0:T(8,128)} %material.1, s32[1,2,4096]{2,1,0:T(2,128)} %own_rows.1, ...), custom_call_target="tpu_custom_call" | custom-call | tf_op jit(solution)/shard_map/coarse/pallas_call | solution.py:427
  55.9 1.7 %assemble.1 = (f32[1,48,48]{2,1,0:T(8,128)}, f32[1,4,48,48]{3,2,1,0:T(8,128)}) custom-call(f32[6,16,128]{2,1,0:T(8,128)} %get-tuple-element.4.whole, f32[3,6,8,128]{3,2,1,0:T(8,128)} %get-tuple-element.5.forward), custom_call_target="tpu_custom_call" | custom-call | tf_op jit(solution)/shard_map/assemble/pallas_call | solution.py:467

commit v5 on v4

--- a/solution.py
+++ b/solution.py
@@ -25,9 +25,11 @@
 SLAB = 4096
 CHUNK = 512
 NCHUNK = SLAB // CHUNK
-BACK = 2
+BACK = 3
 UP = [(1, n) for n in range(NCHUNK - BACK)] + [(0, n) for n in range(NCHUNK)]
 DOWN = [(1, n) for n in range(NCHUNK - BACK, NCHUNK)]
+BEFORE = 3
+PIECE = 16
 FAR_FIRST = (4, 3, 5, 2, 6, 1, 7)
 NLEVEL = 16
 GROUP = 8
@@ -98,16 +100,14 @@
 def kernel(
     counts_in, couple_in, stiffness_in, eigen, material, own_rows, send_rows,
     whole_out, forward_out,
-    counts, couple, stiffness, eig, halo, mat, coef, field, image, table, own_sel, own_kept, send_sel, packed, arrived, down_packed, down_arrived,
+    counts, couple, stiffness, eig, halo, mat, coef, field, image, table, image_rows, own_sel, own_kept, send_sel, packed, arrived, down_packed, down_arrived,
     part, sums, zsums, piece, whole, forward,
     load_sem, halo_send, halo_recv, slab_send, slab_recv, down_send, down_recv,
-    one_send, one_recv, two_send, two_recv, three_send, three_recv, fwd_send, fwd_recv, index_sem, *strips,
+    one_send, one_recv, two_send, two_recv, three_send, three_recv, fwd_send, fwd_recv, index_sem, eigen_sem, *strips,
 ):
     sub, row = lax.axis_index("sub"), lax.axis_index("row")
     z, place = row // GROUP, lax.rem(row, GROUP)
-    barrier, greetings = start_barrier(sub, row)
-
-    loads = [pltpu.make_async_copy(eigen.at[0], eig, load_sem.at[0])]
+    loads = [None]
     own_index = [strips[o * STRIPS : (o + 1) * STRIPS] for o in (0, 1)]
     send_index = [strips[(2 + o) * STRIPS : (3 + o) * STRIPS] for o in (0, 1)]
     index_loads = []
@@ -123,7 +123,15 @@
     loads.append(pltpu.make_async_copy(counts_in, counts, load_sem.at[3 + CX]))
     loads.append(pltpu.make_async_copy(couple_in, couple, load_sem.at[4 + CX]))
     loads.append(pltpu.make_async_copy(stiffness_in, stiffness, load_sem.at[5 + CX]))
-    for load in loads + index_loads[0] + index_loads[1]:
+    def eigen_load(c, p):
+        return pltpu.make_async_copy(eigen.at[0, :, c, p], eig.at[:, c, p], eigen_sem.at[c * CX + p])
+
+    loads[3 + CX].start()
+    for c in range(C):
+        for p in range(CX):
+            eigen_load(c, p).start()
+    barrier, greetings = start_barrier(sub, row)
+    for load in index_loads[0] + loads[1 : 3 + CX] + loads[4 + CX :] + index_loads[1]:
         load.start()
     loads[3 + CX].wait()
     count = counts[0]
@@ -139,44 +147,44 @@
     def _():
         halo[1] = jnp.zeros((K, C, GY, GZ), BF16)
 
-    loads[0].wait()
-
-    def mask_column(k, carry):
-        keep = kept(k)
-        for c in range(C):
-            for p in range(CX):
-                base = pl.multiple_of(k * (C * CX * GY) + (c * CX + p) * GY, GY)
-                field[pl.ds(base, GY), :] = eig[k, c, p].astype(F32) * keep
-        return carry
-
-    lax.fori_loop(0, K, mask_column, 0)
-
     def across(source, at):
         return source[pl.ds(at, K, stride=C * CX * GY), :]
 
     def fill_table(block, carry):
+        c, p = block // CX, lax.rem(block, CX)
+        eigen_load(c, p).wait()
+        for k in range(K):
+            base = pl.multiple_of(k * (C * CX * GY) + block * GY, GY)
+            field[pl.ds(base, GY), :] = eig[k, c, p].astype(F32) * keeps[k]
         for y in range(GY):
             at = block * GY + y
             table[pl.ds(pl.multiple_of(at * GZ, GZ), GZ), :] = widen(across(field, at).T)
         return carry
 
-    lax.fori_loop(0, C * CX, fill_table, 0)
+    keeps = [kept(k) for k in range(K)]
+    lax.fori_loop(0, BEFORE, fill_table, 0)
 
     pl.semaphore_wait(barrier, greetings)
-    up = pltpu.make_async_remote_copy(
-        src_ref=eigen.at[0, :, :, CX - 1], dst_ref=halo.at[0], send_sem=halo_send.at[0],
-        recv_sem=halo_recv.at[0], device_id=(sub, jnp.minimum(row + 1, NROW - 1)), device_id_type=MESH)
-    down = pltpu.make_async_remote_copy(
-        src_ref=eigen.at[0, :, :, 0], dst_ref=halo.at[1], send_sem=halo_send.at[1],
-        recv_sem=halo_recv.at[1], device_id=(sub, jnp.maximum(row - 1, 0)), device_id_type=MESH)
-
-    @pl.when(row < NROW - 1)
-    def _():
-        up.start()
-
-    @pl.when(row > 0)
-    def _():
-        down.start()
+    def piece_of(h, side, to):
+        some = pl.ds(h * PIECE, PIECE)
+        return pltpu.make_async_remote_copy(
+            src_ref=eigen.at[0, some, :, (CX - 1) * (1 - side)], dst_ref=halo.at[side, some],
+            send_sem=halo_send.at[side, h], recv_sem=halo_recv.at[side, h],
+            device_id=(sub, to), device_id_type=MESH)
+
+    pieces = range(K // PIECE)
+    ups = [piece_of(h, 0, jnp.minimum(row + 1, NROW - 1)) for h in pieces]
+    downs_x = [piece_of(h, 1, jnp.maximum(row - 1, 0)) for h in pieces]
+    for h in pieces:
+        @pl.when(row < NROW - 1)
+        def _(h=h):
+            ups[h].start()
+
+        @pl.when(row > 0)
+        def _(h=h):
+            downs_x[h].start()
+
+    lax.fori_loop(BEFORE, C * CX, fill_table, 0)
 
     for load in index_loads[0]:
         load.wait()
@@ -203,9 +211,6 @@
             device_id=(at_sub(sub, o + 1), row), device_id_type=MESH)
         slab.start()
         slabs.append(slab)
-    for e, (o, n) in enumerate(DOWN):
-        gather(own_index[o], table, own_kept.at[e], n * CHUNK)
-
     for p in range(CX + 2):
         loads[1 + p].wait()
     loads[5 + CX].wait()
@@ -238,14 +243,6 @@
         for c in range(C):
             coef[5 * CX + 1 + C * p + c] = along[0] + along[1] + along[2] + 2.0 * along[c]
 
-    @pl.when(row > 0)
-    def _():
-        up.wait_recv()
-
-    @pl.when(row < NROW - 1)
-    def _():
-        down.wait_recv()
-
     def apply_column(k):
         keep = kept(k)
         for c in range(C):
@@ -271,14 +268,23 @@
             apply_column(4 * block + u)
         return carry
 
-    lax.fori_loop(0, K // 4, apply_columns, 0)
+    for h in pieces:
+        @pl.when(row > 0)
+        def _(h=h):
+            ups[h].wait_recv()
+
+        @pl.when(row < NROW - 1)
+        def _(h=h):
+            downs_x[h].wait_recv()
+
+        lax.fori_loop(h * PIECE // 4, (h + 1) * PIECE // 4, apply_columns, 0)
 
     def image_table(block, total):
         basis, turned = [], []
         for y in range(GY):
             at = block * GY + y
             wide = widen(across(image, at).T)
-            table[pl.ds(pl.multiple_of(at * GZ, GZ), GZ), :] = wide
+            image_rows[pl.ds(pl.multiple_of(at * GZ, GZ), GZ), :] = wide
             turned.append(wide.astype(BF16))
             basis.append(across(field, at).astype(BF16))
         return total + jnp.dot(
@@ -290,7 +296,7 @@
         load.wait()
     downs = []
     for e, (o, n) in enumerate(DOWN):
-        gather(send_index[o], table, own_sel.at[e % 2], n * CHUNK)
+        gather(send_index[o], image_rows, own_sel.at[e % 2], n * CHUNK)
         down_packed[e] = turned(plain, own_sel[e % 2])
         slab = pltpu.make_async_remote_copy(
             src_ref=down_packed.at[e], dst_ref=down_arrived.at[e],
@@ -298,9 +304,12 @@
             device_id=(at_sub(sub, -o - 1), row), device_id_type=MESH)
         slab.start()
         downs.append(slab)
+    for e, (o, n) in enumerate(DOWN):
+        gather(own_index[o], table, own_kept.at[e], n * CHUNK)
+
     pairs = [jnp.zeros((K, LANES), F32) for o in (0, 1)]
     for e, (o, n) in enumerate(UP):
-        gather(send_index[o], table, send_sel.at[e % 2], n * CHUNK)
+        gather(send_index[o], image_rows, send_sel.at[e % 2], n * CHUNK)
         slabs[e].wait_recv()
         pairs[o] = pairs[o] + jnp.dot(
             arrived[e], send_sel[e % 2].astype(BF16), preferred_element_type=F32)
@@ -354,13 +363,14 @@
             send_sem=three_send, recv_sem=three_recv,
             device_id=(sub, z * GROUP + lax.rem(place + step, GROUP)), device_id_type=MESH))
 
-    @pl.when(row < NROW - 1)
-    def _():
-        up.wait_send()
-
-    @pl.when(row > 0)
-    def _():
-        down.wait_send()
+    for h in pieces:
+        @pl.when(row < NROW - 1)
+        def _(h=h):
+            ups[h].wait_send()
+
+        @pl.when(row > 0)
+        def _(h=h):
+            downs_x[h].wait_send()
 
     for slab in slabs + downs:
         slab.wait_send()
@@ -443,6 +453,7 @@
             pltpu.VMEM((K * C * CX * GY, GZ), F32),
             pltpu.VMEM((K * C * CX * GY, GZ), F32),
             pltpu.VMEM((ROWS, LANES), F32),
+            pltpu.VMEM((ROWS, LANES), F32),
             pltpu.VMEM((2, CHUNK, LANES), F32),
             pltpu.VMEM((BACK, CHUNK, LANES), F32),
             pltpu.VMEM((2, CHUNK, LANES), F32),
@@ -456,9 +467,9 @@
             pltpu.VMEM((2, 16, LANES), F32),
             pltpu.VMEM((OWNERS, 16, LANES), F32),
             pltpu.VMEM((3, OWNERS, 8, LANES), F32),
-            dma((6 + CX,)), dma((2,)), dma((2,)), dma((len(UP),)), dma((len(UP),)), dma((BACK,)), dma((BACK,)),
+            dma((6 + CX,)), dma((2, K // PIECE)), dma((2, K // PIECE)), dma((len(UP),)), dma((len(UP),)), dma((BACK,)), dma((BACK,)),
             dma((GROUP,)), dma, dma, dma, dma, dma, dma((3,)), dma,
-            dma((2, 2, STRIPS)),
+            dma((2, 2, STRIPS)), dma((C * CX,)),
         ] + [pltpu.SMEM((STRIP,), jnp.int32) for _ in range(4 * STRIPS)],
         compiler_params=pltpu.CompilerParams(
             collective_id=0, has_side_effects=True, vmem_limit_bytes=60 * 2**20),

time: 57.7 us -> 56.9 us (0.986)
  Pallas kernels: 56.3 us -> 55.4 us
    pallas_call x1, Pallas kernels: 54.6 us -> 53.8 us  [shards(): pl.pallas_call(kernel, out_shape=(jax.ShapeDtypeStruct((OWNERS, 16, LANES...]
where the time goes in v5:
time: 56.9 us; the launch traced here: 56.7 us
  Pallas kernels  55.4 us (97%)
  between operations  1.29 us (2%)
    pallas_call x1, Pallas kernels, shards(): pl.pallas_call(kernel, out_shape=(jax.ShapeDtypeStruct((OWNERS, 16, LANES...  53.8 us
    pallas_call x1, Pallas kernels, shards(): pl.pallas_call(assemble, out_shape=(jax.ShapeDtypeStruct((1, K, K), F32),...  1.68 us

profile of v5, /device:TPU:1, one launch (start us, length us, event | category | flops | bytes accessed | tf_op | source)
XLA Modules:
  0.0 56.7 jit_solution(11125906756205132472)
XLA Ops:
  1.3 53.8 %coarse.1 = (f32[6,16,128]{2,1,0:T(8,128)}, f32[3,6,8,128]{3,2,1,0:T(8,128)}) custom-call(s32[1]{0:T(128)S(6)} %copy.9.counts_in, s32[1,2]{1,0:T(1,128)} %couple_in.1, f32[16]{0:T(128)} %stiffness_in.1, bf16[1,48,3,2,16,128]{5,4,3,2,1,0:T(8,128)(2,1)} %eigen.1, s32[1,128,16,128]{3,2,1,0:T(8,128)} %material.1, s32[1,2,4096]{2,1,0:T(2,128)} %own_rows.1, ...), custom_call_target="tpu_custom_call" | custom-call | tf_op jit(solution)/shard_map/coarse/pallas_call | solution.py:437
  55.0 1.7 %assemble.1 = (f32[1,48,48]{2,1,0:T(8,128)}, f32[1,4,48,48]{3,2,1,0:T(8,128)}) custom-call(f32[6,16,128]{2,1,0:T(8,128)} %get-tuple-element.4.whole, f32[3,6,8,128]{3,2,1,0:T(8,128)} %get-tuple-element.5.forward), custom_call_target="tpu_custom_call" | custom-call | tf_op jit(solution)/shard_map/assemble/pallas_call | solution.py:478

commit v6 on v5

--- a/solution.py
+++ b/solution.py
@@ -450,8 +450,8 @@
             pltpu.VMEM((2, K, C, GY, GZ), BF16),
             pltpu.VMEM((CX + 2, GY, GZ), jnp.int32),
             pltpu.VMEM((5 * CX + 1 + C * CX, GY, GZ), F32),
-            pltpu.VMEM((K * C * CX * GY, GZ), F32),
-            pltpu.VMEM((K * C * CX * GY, GZ), F32),
+            pltpu.VMEM(((K + 1) * C * CX * GY, GZ), F32),
+            pltpu.VMEM(((K + 1) * C * CX * GY, GZ), F32),
             pltpu.VMEM((ROWS, LANES), F32),
             pltpu.VMEM((ROWS, LANES), F32),
             pltpu.VMEM((2, CHUNK, LANES), F32),

time: 56.9 us -> 56.9 us (level)
  no operation moved by 1% of the time
where the time goes in v6:
time: 56.9 us; the launch traced here: 56.7 us
  Pallas kernels  55.4 us (97%)
  between operations  1.29 us (2%)
    pallas_call x1, Pallas kernels, shards(): pl.pallas_call(kernel, out_shape=(jax.ShapeDtypeStruct((OWNERS, 16, LANES...  53.8 us
    pallas_call x1, Pallas kernels, shards(): pl.pallas_call(assemble, out_shape=(jax.ShapeDtypeStruct((1, K, K), F32),...  1.68 us

profile of v6, /device:TPU:1, one launch (start us, length us, event | category | flops | bytes accessed | tf_op | source)
XLA Modules:
  0.0 56.7 jit_solution(1133416885177486125)
XLA Ops:
  1.3 53.8 %coarse.1 = (f32[6,16,128]{2,1,0:T(8,128)}, f32[3,6,8,128]{3,2,1,0:T(8,128)}) custom-call(s32[1]{0:T(128)S(6)} %copy.9.counts_in, s32[1,2]{1,0:T(1,128)} %couple_in.1, f32[16]{0:T(128)} %stiffness_in.1, bf16[1,48,3,2,16,128]{5,4,3,2,1,0:T(8,128)(2,1)} %eigen.1, s32[1,128,16,128]{3,2,1,0:T(8,128)} %material.1, s32[1,2,4096]{2,1,0:T(2,128)} %own_rows.1, ...), custom_call_target="tpu_custom_call" | custom-call | tf_op jit(solution)/shard_map/coarse/pallas_call | solution.py:437
  55.0 1.7 %assemble.1 = (f32[1,48,48]{2,1,0:T(8,128)}, f32[1,4,48,48]{3,2,1,0:T(8,128)}) custom-call(f32[6,16,128]{2,1,0:T(8,128)} %get-tuple-element.4.whole, f32[3,6,8,128]{3,2,1,0:T(8,128)} %get-tuple-element.5.forward), custom_call_target="tpu_custom_call" | custom-call | tf_op jit(solution)/shard_map/assemble/pallas_call | solution.py:478
